TPU v7x, 128 devices: a whole 4x4x4 slice. The times are simulated.
128 devices in a mesh: ctx: 8 (over z, core), head: 16 (over x, y).
Axes of the slice: x: 4, y: 4, z: 4, core: 2. Of those that a mesh axis runs over, the one named last changes fastest.
Arguments:
- values: bfloat16 [16384, 8192], P('ctx', 'head'), may hold values from -6 to 6
- step_sizes: float32 [16384, 128], P('ctx', 'head'), may hold values from 0.5 to 2
- decay_rates: float32 [128], P('head'), may hold values from 3.0517578e-05 to 0.1
- write_keys: bfloat16 [16384, 128], P('ctx'), may hold values from -0.5 to 0.5
- read_keys: bfloat16 [16384, 128], P('ctx'), may hold values from -0.5 to 0.5
- doc_ids: int32 [16384], P('ctx'), may hold values from 0 to 11, never falling along the last dimension, each value on 1 to 8192 neighbouring positions
- out_grad: bfloat16 [16384, 8192], P('ctx', 'head'), may hold values from -6 to 6
Outputs:
- value_grad: bfloat16 [16384, 8192], P('ctx', 'head')
- step_grad: float32 [16384, 128], P('ctx', 'head')
- write_grad: float32 [16384, 128], P(('ctx', 'head'))
- read_grad: float32 [16384, 128], P(('ctx', 'head'))
Inputs may be any that keep to these rules, and one draw needn't show every extreme that they name: `doc_ids`: document numbers never fall along the row, start at 0, and each number forms one run of 1 to 8192 positions; one document has exactly 8192 positions.
All inputs are finite; a program needn't handle non-finite values.
Results may differ from a plain program's by a relative error of at most 0.001.
Values sent between devices are 32-bit elements; how exact they have to be, the bound alone decides.
A program may use at most 128 MiB of HBM per device.

v0:
```python
from functools import partial

import jax
import jax.numpy as jnp
from jax import lax
from jax.sharding import PartitionSpec as P

QCHUNK = 256


def from_behind(value, axis, steps):
    count = lax.axis_size(axis)
    initial, last = (max(0, -steps), min(count, count - steps))
    return lax.ppermute(value, axis, [(source, source + steps) for source in range(initial, last)])


def group_step(hidden_state, pieces, decay_rates):
    inputs, step_sizes, write_keys, read_keys, doc_starts = pieces
    highest = lax.Precision.HIGHEST
    length = inputs.shape[0]
    cumulative = jnp.cumsum(-step_sizes * decay_rates[None, :], axis=0).T
    doc_count = jnp.cumsum(doc_starts)
    rows = lax.broadcasted_iota(jnp.int32, (length, length), 0)
    cols = lax.broadcasted_iota(jnp.int32, (length, length), 1)
    same_doc = (doc_count[:, None] == doc_count[None, :]) & (rows >= cols)
    spread = jnp.where(same_doc[None], cumulative[:, :, None] - cumulative[:, None, :], 0.0)
    decays = jnp.where(same_doc[None], jnp.exp(spread), 0.0)
    scores = jnp.dot(read_keys, write_keys.T, precision=highest)
    weights = decays * scores[None] * step_sizes.T[:, None, :]
    output = jnp.einsum("hts,shp->thp", weights, inputs, precision=highest)
    reach = jnp.where((doc_count == 0)[None, :], jnp.exp(cumulative), 0.0)
    output = output + reach.T[:, :, None] * jnp.einsum(
        "tn,hnp->thp", read_keys, hidden_state, precision=highest
    )
    to_end = decays[:, -1, :] * step_sizes.T
    next_state = jnp.einsum(
        "sn,shp->hnp", write_keys, to_end.T[:, :, None] * inputs, precision=highest
    )
    next_state = next_state + reach[:, -1][:, None, None] * hidden_state
    return (next_state, output)


def span_forward(
    inputs, step_sizes, write_keys, read_keys, doc_starts, hidden_state, decay_rates, block_len
):
    total = inputs.shape[0]
    blocks = total // block_len
    heads = inputs.shape[1]
    width = inputs.shape[2]
    states = write_keys.shape[1]
    pieces = (
        inputs.reshape(blocks, block_len, heads, width),
        step_sizes.reshape(blocks, block_len, heads),
        write_keys.reshape(blocks, block_len, states),
        read_keys.reshape(blocks, block_len, states),
        doc_starts.reshape(blocks, block_len),
    )
    stepper = jax.checkpoint(partial(group_step, decay_rates=decay_rates))
    final, outputs = lax.scan(stepper, hidden_state, pieces)
    return (outputs.reshape(total, heads, width), final)


def shards(values, step_sizes, decay_rates, write_keys, read_keys, doc_ids, out_grad):
    highest = lax.Precision.HIGHEST
    heads_here = decay_rates.shape[0]
    length = values.shape[0]
    head_size = values.shape[1] // heads_here
    state_size = write_keys.shape[1]
    inputs = values.astype(jnp.float32).reshape(length, heads_here, head_size)
    cotangent = out_grad.astype(jnp.float32).reshape(length, heads_here, head_size)
    writes = write_keys.astype(jnp.float32)
    reads = read_keys.astype(jnp.float32)
    prior = from_behind(doc_ids[-1:], "ctx", 1)
    doc_starts = jnp.concatenate(
        [
            (doc_ids[:1] != prior).astype(jnp.float32),
            (doc_ids[1:] != doc_ids[:-1]).astype(jnp.float32),
        ]
    )
    empty = jnp.zeros((heads_here, state_size, head_size), jnp.float32)
    unused, local_end = span_forward(
        inputs, step_sizes, writes, reads, doc_starts, empty, decay_rates, QCHUNK
    )
    log_decay = -step_sizes * decay_rates[None, :]
    reach = jnp.where(
        (jnp.cumsum(doc_starts) == 0)[:, None], jnp.exp(jnp.cumsum(log_decay, axis=0)), 0.0
    )
    through = jnp.where(jnp.sum(doc_starts) == 0, jnp.exp(jnp.sum(log_decay, axis=0)), 0.0)
    back_local = jnp.einsum("tn,thp->hnp", reads, reach[:, :, None] * cotangent, precision=highest)

    def forward_turn(index_step, carried):
        return from_behind(through[:, None, None] * carried + local_end, "ctx", 1)

    def backward_turn(index_step, carried):
        return from_behind(through[:, None, None] * carried + back_local, "ctx", -1)

    state_in = lax.fori_loop(0, lax.axis_size("ctx") - 1, forward_turn, empty)
    end_grad = lax.fori_loop(0, lax.axis_size("ctx") - 1, backward_turn, empty)

    def forward(inputs_in, steps_in, writes_in, reads_in):
        return span_forward(
            inputs_in, steps_in, writes_in, reads_in, doc_starts, state_in, decay_rates, QCHUNK
        )

    outputs, pullback = jax.vjp(forward, inputs, step_sizes, writes, reads)
    grads = pullback((cotangent, end_grad))
    value_grad = grads[0].reshape(length, heads_here * head_size).astype(jnp.bfloat16)
    write_grad, read_grad = (
        lax.psum_scatter(grads[2], "head", scatter_dimension=0, tiled=True),
        lax.psum_scatter(grads[3], "head", scatter_dimension=0, tiled=True),
    )
    return (value_grad, grads[1], write_grad, read_grad)


def solution(mesh):
    return jax.shard_map(
        shards,
        mesh=mesh,
        in_specs=(
            P("ctx", "head"),
            P("ctx", "head"),
            P("head"),
            P("ctx", None),
            P("ctx", None),
            P("ctx"),
            P("ctx", "head"),
        ),
        out_specs=(
            P("ctx", "head"),
            P("ctx", "head"),
            P(("ctx", "head"), None),
            P(("ctx", "head"), None),
        ),
        check_vma=False,
    )
```

profile of v0, /device:TPU:0, one launch (start us, length us, event | category | flops | bytes accessed | tf_op | source)
XLA Modules:
  0.0 637.8 jit_solution(14330345019721246310)
XLA Ops:
  11.7 3.9 copy.47
  15.6 4.1 convert_element_type.20
  22.7 6.7 %reshape.638 = f32[8,256,8,64]{3,2,1,0:T(8,128)} reshape(bf16[2048,512]{1,0:T(8,128)(2,1)} %param.17) | data formatting | bytes 6291456 | tf_op jit(solution)/shard_map/reshape;reshape | solution.py:52
  29.4 6.9 %copy.50 = f32[8,256,8,64]{1,3,2,0:T(8,128)} copy(f32[8,256,8,64]{3,2,1,0:T(8,128)} %reshape.638) | data formatting | bytes 8388608
  37.4 6.1 copy.66
  45.5 4.3 fusion.87
  50.6 69.4 %while.68 = (s32[]{:T(128)}, f32[8,128,64]{2,1,0:T(8,128)S(1)}, f32[8]{0:T(128)S(1)}, f32[8,128,64]{2,1,0:T(8,128)S(1)}, s32[]{:T(128)}) while((s32[]{:T(128)}, f32[8,128,64]{2,1,0:T(8,128)S(1)}, f32[8]{0:T(128)S(1)}, f32[8,128,64]{2,1,0:T(8,128)S(1)}, s32[]{:T(128)}) %tuple.164), condition=%wide.region_7.8_spmd, body=%wide.region_6.7_spmd.sunk | while | flops 131074 | bytes 1835141 | solution.py:98
  52.0 4.2 collective-permute-done
  57.6 9.2 %collective-permute-done = f32[8,128,64]{2,1,0:T(8,128)S(1)} collective-permute-done((f32[8,128,64]{2,1,0:T(8,128)S(1)}, f32[8,128,64]{2,1,0:T(8,128)S(1)}, u32[]{:S(2)}, u32[]{:S(2)}) %collective-permute-start) | collective-permute-done | bytes 262176 | tf_op jit(solution)/shard_map/while/body/eval_jaxpr/ppermute | solution.py:14
  68.3 9.2 %collective-permute-done = f32[8,128,64]{2,1,0:T(8,128)S(1)} collective-permute-done((f32[8,128,64]{2,1,0:T(8,128)S(1)}, f32[8,128,64]{2,1,0:T(8,128)S(1)}, u32[]{:S(2)}, u32[]{:S(2)}) %collective-permute-start) | collective-permute-done | bytes 262176 | tf_op jit(solution)/shard_map/while/body/eval_jaxpr/ppermute | solution.py:14
  78.9 9.2 %collective-permute-done = f32[8,128,64]{2,1,0:T(8,128)S(1)} collective-permute-done((f32[8,128,64]{2,1,0:T(8,128)S(1)}, f32[8,128,64]{2,1,0:T(8,128)S(1)}, u32[]{:S(2)}, u32[]{:S(2)}) %collective-permute-start) | collective-permute-done | bytes 262176 | tf_op jit(solution)/shard_map/while/body/eval_jaxpr/ppermute | solution.py:14
  89.5 9.2 %collective-permute-done = f32[8,128,64]{2,1,0:T(8,128)S(1)} collective-permute-done((f32[8,128,64]{2,1,0:T(8,128)S(1)}, f32[8,128,64]{2,1,0:T(8,128)S(1)}, u32[]{:S(2)}, u32[]{:S(2)}) %collective-permute-start) | collective-permute-done | bytes 262176 | tf_op jit(solution)/shard_map/while/body/eval_jaxpr/ppermute | solution.py:14
  100.1 9.2 %collective-permute-done = f32[8,128,64]{2,1,0:T(8,128)S(1)} collective-permute-done((f32[8,128,64]{2,1,0:T(8,128)S(1)}, f32[8,128,64]{2,1,0:T(8,128)S(1)}, u32[]{:S(2)}, u32[]{:S(2)}) %collective-permute-start) | collective-permute-done | bytes 262176 | tf_op jit(solution)/shard_map/while/body/eval_jaxpr/ppermute | solution.py:14
  110.7 9.2 %collective-permute-done = f32[8,128,64]{2,1,0:T(8,128)S(1)} collective-permute-done((f32[8,128,64]{2,1,0:T(8,128)S(1)}, f32[8,128,64]{2,1,0:T(8,128)S(1)}, u32[]{:S(2)}, u32[]{:S(2)}) %collective-permute-start) | collective-permute-done | bytes 262176 | tf_op jit(solution)/shard_map/while/body/eval_jaxpr/ppermute | solution.py:14
  120.1 39.9 %while.72 = (s32[]{:T(128)}, f32[8,128,64]{1,2,0:T(8,128)S(1)}, f32[8,256]{1,0:T(8,128)S(1)}, f32[8,256,8]{1,2,0:T(8,128)S(1)}, f32[8]{0:T(128)S(1)}, /*index=5*...) while((s32[]{:T(128)}, f32[8,128,64]{1,2,0:T(8,128)S(1)}, ...), condition=%wide.region_13.14_spmd.clone, body=%wide.region_8.13_spmd.clone.sunk | while | flops 202158368 | bytes 1338257 | solution.py:59
  160.3 72.0 %while.69 = (s32[]{:T(128)}, f32[8,128,64]{2,1,0:T(8,128)S(1)}, f32[8]{0:T(128)S(1)}, f32[8,128,64]{2,1,0:T(8,128)S(1)}, s32[]{:T(128)}) while((s32[]{:T(128)}, f32[8,128,64]{2,1,0:T(8,128)S(1)}, f32[8]{0:T(128)S(1)}, f32[8,128,64]{2,1,0:T(8,128)S(1)}, s32[]{:T(128)}) %tuple.196), condition=%wide.region_15.16_spmd, body=%wide.region_14.15_spmd.sunk | while | flops 131074 | bytes 1835141 | solution.py:97
  160.5 9.1 %collective-permute-start.1 = (f32[8,128,64]{2,1,0:T(8,128)S(1)}, f32[8,128,64]{2,1,0:T(8,128)S(1)}, u32[]{:S(2)}, u32[]{:S(2)}) collective-permute-start(f32[8,128,64]{2,1,0:T(8,128)S(1)} %multiply_add_fusion.5), channel_id=1, source_target_pairs={{0,16},{16,32},{32,48},{48,64},{64,80},{80,96},{96,112},{1,17},{17... | collective-permute-start | bytes 786440 | tf_op jit(solution)/shard_map/while/body/eval_jaxpr/ppermute | solution.py:14
  171.2 6.5 %collective-permute-start.1 = (f32[8,128,64]{2,1,0:T(8,128)S(1)}, f32[8,128,64]{2,1,0:T(8,128)S(1)}, u32[]{:S(2)}, u32[]{:S(2)}) collective-permute-start(f32[8,128,64]{2,1,0:T(8,128)S(1)} %multiply_add_fusion.5), channel_id=1, source_target_pairs={{0,16},{16,32},{32,48},{48,64},{64,80},{80,96},{96,112},{1,17},{17... | collective-permute-start | bytes 786440 | tf_op jit(solution)/shard_map/while/body/eval_jaxpr/ppermute | solution.py:14
  179.4 9.0 %collective-permute-start.1 = (f32[8,128,64]{2,1,0:T(8,128)S(1)}, f32[8,128,64]{2,1,0:T(8,128)S(1)}, u32[]{:S(2)}, u32[]{:S(2)}) collective-permute-start(f32[8,128,64]{2,1,0:T(8,128)S(1)} %multiply_add_fusion.5), channel_id=1, source_target_pairs={{0,16},{16,32},{32,48},{48,64},{64,80},{80,96},{96,112},{1,17},{17... | collective-permute-start | bytes 786440 | tf_op jit(solution)/shard_map/while/body/eval_jaxpr/ppermute | solution.py:14
  190.0 9.0 %collective-permute-start.1 = (f32[8,128,64]{2,1,0:T(8,128)S(1)}, f32[8,128,64]{2,1,0:T(8,128)S(1)}, u32[]{:S(2)}, u32[]{:S(2)}) collective-permute-start(f32[8,128,64]{2,1,0:T(8,128)S(1)} %multiply_add_fusion.5), channel_id=1, source_target_pairs={{0,16},{16,32},{32,48},{48,64},{64,80},{80,96},{96,112},{1,17},{17... | collective-permute-start | bytes 786440 | tf_op jit(solution)/shard_map/while/body/eval_jaxpr/ppermute | solution.py:14
  200.6 9.0 %collective-permute-start.1 = (f32[8,128,64]{2,1,0:T(8,128)S(1)}, f32[8,128,64]{2,1,0:T(8,128)S(1)}, u32[]{:S(2)}, u32[]{:S(2)}) collective-permute-start(f32[8,128,64]{2,1,0:T(8,128)S(1)} %multiply_add_fusion.5), channel_id=1, source_target_pairs={{0,16},{16,32},{32,48},{48,64},{64,80},{80,96},{96,112},{1,17},{17... | collective-permute-start | bytes 786440 | tf_op jit(solution)/shard_map/while/body/eval_jaxpr/ppermute | solution.py:14
  211.2 9.0 %collective-permute-start.1 = (f32[8,128,64]{2,1,0:T(8,128)S(1)}, f32[8,128,64]{2,1,0:T(8,128)S(1)}, u32[]{:S(2)}, u32[]{:S(2)}) collective-permute-start(f32[8,128,64]{2,1,0:T(8,128)S(1)} %multiply_add_fusion.5), channel_id=1, source_target_pairs={{0,16},{16,32},{32,48},{48,64},{64,80},{80,96},{96,112},{1,17},{17... | collective-permute-start | bytes 786440 | tf_op jit(solution)/shard_map/while/body/eval_jaxpr/ppermute | solution.py:14
  221.9 9.0 %collective-permute-start.1 = (f32[8,128,64]{2,1,0:T(8,128)S(1)}, f32[8,128,64]{2,1,0:T(8,128)S(1)}, u32[]{:S(2)}, u32[]{:S(2)}) collective-permute-start(f32[8,128,64]{2,1,0:T(8,128)S(1)} %multiply_add_fusion.5), channel_id=1, source_target_pairs={{0,16},{16,32},{32,48},{48,64},{64,80},{80,96},{96,112},{1,17},{17... | collective-permute-start | bytes 786440 | tf_op jit(solution)/shard_map/while/body/eval_jaxpr/ppermute | solution.py:14
  232.5 45.7 %while.71 = (s32[]{:T(128)}, f32[8,128,64]{1,2,0:T(8,128)S(1)}, f32[8,8,128,64]{2,3,1,0:T(8,128)}, f32[8,256]{1,0:T(8,128)S(1)}, f32[8,256,8]{1,2,0:T(8,128)S(1)...) while((s32[]{:T(128)}, f32[8,128,64]{1,2,0:T(8,128)S(1)}, ...), condition=%wide.region_21.22_spmd.clone, body=%wide.region_16.21_spmd.clone.sunk | while | flops 202092832 | bytes 1862028 | solution.py:59
  282.1 189.7 %while.70 = (s32[]{:T(128)}, f32[8,128,64]{1,2,0:T(8,128)S(1)}, bf16[8,256,8,64]{1,3,2,0:T(8,128)(2,1)}, f32[8,256,8]{1,2,0:T(8,128)S(1)}, f32[8,256,128]{2,1,0:...) while((s32[]{:T(128)}, f32[8,128,64]{1,2,0:T(8,128)S(1)}, ...), condition=%wide.region_36.37_spmd, body=%wide.region_22.36_spmd.sunk | while | flops 2127157504 | bytes 18016940 | solution.py:59
  290.5 3.9 fusion.170
  296.3 2.7 fusion.171
  306.7 2.6 constant_dynamic-slice_fusion.8
  314.3 3.9 fusion.170
  320.0 2.7 fusion.171
  330.5 2.6 constant_dynamic-slice_fusion.8
  338.0 3.9 fusion.170
  343.8 2.7 fusion.171
  354.2 2.6 constant_dynamic-slice_fusion.8
  361.7 3.9 fusion.170
  367.5 2.7 fusion.171
  385.4 3.9 fusion.170
  391.2 2.7 fusion.171
  409.1 3.9 fusion.170
  414.9 2.7 fusion.171
  432.8 3.9 fusion.170
  438.6 2.7 fusion.171
  456.6 3.9 fusion.170
  462.3 2.7 fusion.171
  473.4 3.6 copy.59
  477.0 6.4 %reshape.637 = bf16[2048,512]{1,0:T(8,128)(2,1)} reshape(bf16[8,256,8,64]{3,2,1,0:T(8,128)(2,1)} %copy.59) | data formatting | bytes 4194304
  483.5 71.1 %reduce-scatter.3.cloned.1.call-done = f32[128,128]{1,0:T(8,128)} async-done(((f32[2048,128]{1,0:T(8,128)}), f32[128,128]{1,0:T(8,128)}) %reduce-scatter.3.cloned.1.call-update) | async-done | bytes 65552 | tf_op jit(solution)/shard_map/reduce_scatter | solution.py:109
  554.6 76.3 %reduce-scatter.5.cloned.1.call-done = f32[128,128]{1,0:T(8,128)} async-done(((f32[2048,128]{1,0:T(8,128)}), f32[128,128]{1,0:T(8,128)}) %reduce-scatter.5.cloned.1.call-update) | async-done | bytes 65552 | tf_op jit(solution)/shard_map/reduce_scatter | solution.py:110
  (699 shorter events, 249.8 us)
Async XLA Ops:
  7.2 547.5 %reduce-scatter.3.cloned.1.call-start = ((), (), s32[]{:S(2)}) async-start(), calls=%async_computation.2 | async-start | bytes 1114112 | tf_op jit(solution)/shard_map/reduce_scatter | solution.py:109
  8.5 35.0 %collective-permute-start.2 = (s32[1]{0:T(128)}, s32[1]{0:T(128)}, u32[]{:S(2)}, u32[]{:S(2)}) collective-permute-start(s32[1]{0:T(128)} %get-tuple-element.745), channel_id=1, source_target_pairs={{0,16},{16,32},{32,48},{48,64},{64,80},{80,96},{96,112},{1,17},{17... | collective-permute-start | bytes 20 | tf_op jit(solution)/shard_map/ppermute | solution.py:14
  15.6 4.1 copy-start.2
  15.6 4.1 copy-start.4
  29.4 6.9 %copy-start.3 = (bf16[2048,128]{1,0:T(8,128)(2,1)S(1)}, bf16[2048,128]{1,0:T(8,128)(2,1)}, u32[]{:S(2)}) copy-start(bf16[2048,128]{1,0:T(8,128)(2,1)} %param.20) | copy-start | bytes 1572868
  29.4 7.0 %copy-start.1 = (bf16[2048,128]{1,0:T(8,128)(2,1)S(1)}, bf16[2048,128]{1,0:T(8,128)(2,1)}, u32[]{:S(2)}) copy-start(bf16[2048,128]{1,0:T(8,128)(2,1)} %param.21) | copy-start | bytes 1572868
  50.7 5.5 collective-permute-start
  56.3 10.5 %collective-permute-start = (f32[8,128,64]{2,1,0:T(8,128)S(1)}, f32[8,128,64]{2,1,0:T(8,128)S(1)}, u32[]{:S(2)}, u32[]{:S(2)}) collective-permute-start(f32[8,128,64]{2,1,0:T(8,128)S(1)} %multiply_add_fusion.4), channel_id=1, source_target_pairs={{16,0},{32,16},{48,32},{64,48},{80,64},{96,80},{112,96},{17,1},{33... | collective-permute-start | bytes 786440 | tf_op jit(solution)/shard_map/while/body/eval_jaxpr/ppermute | solution.py:14
  67.0 10.5 %collective-permute-start = (f32[8,128,64]{2,1,0:T(8,128)S(1)}, f32[8,128,64]{2,1,0:T(8,128)S(1)}, u32[]{:S(2)}, u32[]{:S(2)}) collective-permute-start(f32[8,128,64]{2,1,0:T(8,128)S(1)} %multiply_add_fusion.4), channel_id=1, source_target_pairs={{16,0},{32,16},{48,32},{64,48},{80,64},{96,80},{112,96},{17,1},{33... | collective-permute-start | bytes 786440 | tf_op jit(solution)/shard_map/while/body/eval_jaxpr/ppermute | solution.py:14
  77.6 10.5 %collective-permute-start = (f32[8,128,64]{2,1,0:T(8,128)S(1)}, f32[8,128,64]{2,1,0:T(8,128)S(1)}, u32[]{:S(2)}, u32[]{:S(2)}) collective-permute-start(f32[8,128,64]{2,1,0:T(8,128)S(1)} %multiply_add_fusion.4), channel_id=1, source_target_pairs={{16,0},{32,16},{48,32},{64,48},{80,64},{96,80},{112,96},{17,1},{33... | collective-permute-start | bytes 786440 | tf_op jit(solution)/shard_map/while/body/eval_jaxpr/ppermute | solution.py:14
  88.2 10.5 %collective-permute-start = (f32[8,128,64]{2,1,0:T(8,128)S(1)}, f32[8,128,64]{2,1,0:T(8,128)S(1)}, u32[]{:S(2)}, u32[]{:S(2)}) collective-permute-start(f32[8,128,64]{2,1,0:T(8,128)S(1)} %multiply_add_fusion.4), channel_id=1, source_target_pairs={{16,0},{32,16},{48,32},{64,48},{80,64},{96,80},{112,96},{17,1},{33... | collective-permute-start | bytes 786440 | tf_op jit(solution)/shard_map/while/body/eval_jaxpr/ppermute | solution.py:14
  98.8 10.5 %collective-permute-start = (f32[8,128,64]{2,1,0:T(8,128)S(1)}, f32[8,128,64]{2,1,0:T(8,128)S(1)}, u32[]{:S(2)}, u32[]{:S(2)}) collective-permute-start(f32[8,128,64]{2,1,0:T(8,128)S(1)} %multiply_add_fusion.4), channel_id=1, source_target_pairs={{16,0},{32,16},{48,32},{64,48},{80,64},{96,80},{112,96},{17,1},{33... | collective-permute-start | bytes 786440 | tf_op jit(solution)/shard_map/while/body/eval_jaxpr/ppermute | solution.py:14
  109.4 10.5 %collective-permute-start = (f32[8,128,64]{2,1,0:T(8,128)S(1)}, f32[8,128,64]{2,1,0:T(8,128)S(1)}, u32[]{:S(2)}, u32[]{:S(2)}) collective-permute-start(f32[8,128,64]{2,1,0:T(8,128)S(1)} %multiply_add_fusion.4), channel_id=1, source_target_pairs={{16,0},{32,16},{48,32},{64,48},{80,64},{96,80},{112,96},{17,1},{33... | collective-permute-start | bytes 786440 | tf_op jit(solution)/shard_map/while/body/eval_jaxpr/ppermute | solution.py:14
  160.5 10.6 %collective-permute-start.1 = (f32[8,128,64]{2,1,0:T(8,128)S(1)}, f32[8,128,64]{2,1,0:T(8,128)S(1)}, u32[]{:S(2)}, u32[]{:S(2)}) collective-permute-start(f32[8,128,64]{2,1,0:T(8,128)S(1)} %multiply_add_fusion.5), channel_id=1, source_target_pairs={{0,16},{16,32},{32,48},{48,64},{64,80},{80,96},{96,112},{1,17},{17... | collective-permute-start | bytes 786440 | tf_op jit(solution)/shard_map/while/body/eval_jaxpr/ppermute | solution.py:14
  171.2 8.0 %collective-permute-start.1 = (f32[8,128,64]{2,1,0:T(8,128)S(1)}, f32[8,128,64]{2,1,0:T(8,128)S(1)}, u32[]{:S(2)}, u32[]{:S(2)}) collective-permute-start(f32[8,128,64]{2,1,0:T(8,128)S(1)} %multiply_add_fusion.5), channel_id=1, source_target_pairs={{0,16},{16,32},{32,48},{48,64},{64,80},{80,96},{96,112},{1,17},{17... | collective-permute-start | bytes 786440 | tf_op jit(solution)/shard_map/while/body/eval_jaxpr/ppermute | solution.py:14
  179.4 10.5 %collective-permute-start.1 = (f32[8,128,64]{2,1,0:T(8,128)S(1)}, f32[8,128,64]{2,1,0:T(8,128)S(1)}, u32[]{:S(2)}, u32[]{:S(2)}) collective-permute-start(f32[8,128,64]{2,1,0:T(8,128)S(1)} %multiply_add_fusion.5), channel_id=1, source_target_pairs={{0,16},{16,32},{32,48},{48,64},{64,80},{80,96},{96,112},{1,17},{17... | collective-permute-start | bytes 786440 | tf_op jit(solution)/shard_map/while/body/eval_jaxpr/ppermute | solution.py:14
  190.0 10.5 %collective-permute-start.1 = (f32[8,128,64]{2,1,0:T(8,128)S(1)}, f32[8,128,64]{2,1,0:T(8,128)S(1)}, u32[]{:S(2)}, u32[]{:S(2)}) collective-permute-start(f32[8,128,64]{2,1,0:T(8,128)S(1)} %multiply_add_fusion.5), channel_id=1, source_target_pairs={{0,16},{16,32},{32,48},{48,64},{64,80},{80,96},{96,112},{1,17},{17... | collective-permute-start | bytes 786440 | tf_op jit(solution)/shard_map/while/body/eval_jaxpr/ppermute | solution.py:14
  200.6 10.5 %collective-permute-start.1 = (f32[8,128,64]{2,1,0:T(8,128)S(1)}, f32[8,128,64]{2,1,0:T(8,128)S(1)}, u32[]{:S(2)}, u32[]{:S(2)}) collective-permute-start(f32[8,128,64]{2,1,0:T(8,128)S(1)} %multiply_add_fusion.5), channel_id=1, source_target_pairs={{0,16},{16,32},{32,48},{48,64},{64,80},{80,96},{96,112},{1,17},{17... | collective-permute-start | bytes 786440 | tf_op jit(solution)/shard_map/while/body/eval_jaxpr/ppermute | solution.py:14
  211.2 10.5 %collective-permute-start.1 = (f32[8,128,64]{2,1,0:T(8,128)S(1)}, f32[8,128,64]{2,1,0:T(8,128)S(1)}, u32[]{:S(2)}, u32[]{:S(2)}) collective-permute-start(f32[8,128,64]{2,1,0:T(8,128)S(1)} %multiply_add_fusion.5), channel_id=1, source_target_pairs={{0,16},{16,32},{32,48},{48,64},{64,80},{80,96},{96,112},{1,17},{17... | collective-permute-start | bytes 786440 | tf_op jit(solution)/shard_map/while/body/eval_jaxpr/ppermute | solution.py:14
  221.9 10.5 %collective-permute-start.1 = (f32[8,128,64]{2,1,0:T(8,128)S(1)}, f32[8,128,64]{2,1,0:T(8,128)S(1)}, u32[]{:S(2)}, u32[]{:S(2)}) collective-permute-start(f32[8,128,64]{2,1,0:T(8,128)S(1)} %multiply_add_fusion.5), channel_id=1, source_target_pairs={{0,16},{16,32},{32,48},{48,64},{64,80},{80,96},{96,112},{1,17},{17... | collective-permute-start | bytes 786440 | tf_op jit(solution)/shard_map/while/body/eval_jaxpr/ppermute | solution.py:14
  471.8 5.3 copy-start.5
  471.8 1.6 copy-start
  471.8 159.1 %reduce-scatter.5.cloned.1.call-start = ((), (), s32[]{:S(2)}) async-start(), calls=%async_computation.3 | async-start | bytes 1114112 | tf_op jit(solution)/shard_map/reduce_scatter | solution.py:110
Sparse Core Ops, SparseCore 0:
  471.9 82.6 reduce-scatter.2
  558.7 72.1 reduce-scatter.4
where the time goes:
time: 641 us; the launch traced here: 638 us
  waiting for transfers between devices  218 us (34%)
  matrix products  137 us (21%)
  local copies, waits for them, and re-layouts  114 us (18%)
  other arithmetic  79.5 us (12%)
  starting transfers between devices  71.6 us (11%)
  between operations  16 us (2%)
    reduce_scatter x1, waiting for transfers between devices, shards(): lax.psum_scatter(grads[3], 'head', scatter_dimension=0, tiled=True)  76.3 us
    ppermute x15, starting transfers between devices, from_behind(): lax.ppermute(value, axis, [(source, source + steps) for source in range(i...  71.6 us
    reduce_scatter x1, waiting for transfers between devices, shards(): lax.psum_scatter(grads[2], 'head', scatter_dimension=0, tiled=True)  71.1 us
    ppermute x15, waiting for transfers between devices, from_behind(): lax.ppermute(value, axis, [(source, source + steps) for source in range(i...  69.8 us
    dot_general x16, matrix products, group_step(): output = jnp.einsum('hts,shp->thp', weights, inputs, precision=highest)  52.8 us
    another operation x166, other arithmetic  49.5 us
    dot_general x32, matrix products, group_step(): jnp.einsum('sn,shp->hnp', write_keys, to_end.T[:, :, None] * inputs, prec...  40.2 us
    unnamed x18, local copies, waits for them, and re-layouts  28 us
  transfers between devices with their start and end apart: 17, of which 16 were waited for; matrix products, arithmetic and copies ran while one was open for 7% of the time, Pallas kernels for 0%

commit v1 on v0

v1 whole, which is shorter than its diff:
```python
from functools import partial

import jax
import jax.numpy as jnp
from jax import lax
from jax.experimental import pallas as pl
from jax.experimental.pallas import tpu as pltpu
from jax.sharding import PartitionSpec as P

QCHUNK = 256
ROUNDS = 3
F32 = jnp.float32
BF16 = jnp.bfloat16


def two_parts(value):
    high = value.astype(BF16)
    return high, (value - high.astype(F32)).astype(BF16)


def three_parts(value):
    high = value.astype(BF16)
    rest = value - high.astype(F32)
    middle = rest.astype(BF16)
    return high, middle, (rest - middle.astype(F32)).astype(BF16)


def dot(left, right, contract):
    return lax.dot_general(left, right, ((contract[:1], contract[1:]), ((), ())), preferred_element_type=F32)


def dot_nn(left, right):
    return dot(left, right, (1, 0))


def dot_nt(left, right):
    return dot(left, right, (1, 1))


def dot_tn(left, right):
    return dot(left, right, (0, 0))


def mod(value, count):
    return lax.rem(value + count, count)


def kernel(
    n_ctx, n_head, x_ref, g_ref, step_ref, rate_ref, w_ref, r_ref, doc_ref,
    vg_ref, sg_ref, wg_ref, rg_ref,
    xhi, xlo, ghi, glo, scale, out_acc, val_acc, doc_col, rw, rw_in,
    state, back, half, phi_f, phi_b, sphi, splo, bphi, bplo,
    f_send, f_recv, b_send, b_recv, ctx_ss, ctx_rs, rw_ss, rw_rs,
):
    length, width = x_ref.shape
    heads = step_ref.shape[0]
    head_size = width // heads
    states = w_ref.shape[1]
    q = QCHUNK
    chunks = length // q
    block = length // n_head
    per = q // block
    lanes = 128
    doc_rows = q // lanes
    me_ctx, me = lax.axis_index("ctx"), lax.axis_index("head")

    barrier = pltpu.get_barrier_semaphore()
    for step in (1, 2):
        for side in (step, n_ctx - step):
            pl.semaphore_signal(barrier, inc=1, device_id={"ctx": mod(me_ctx + side, n_ctx)})

    @pl.loop(1, n_head)
    def _(o):
        pl.semaphore_signal(barrier, inc=1, device_id={"head": mod(me + o, n_head)})

    head_rows = lax.broadcasted_iota(jnp.int32, (heads, width), 0)
    head_lanes = lax.broadcasted_iota(jnp.int32, (heads, width), 1)
    of_head = jnp.where(head_lanes // head_size == head_rows, 1.0, 0.0)
    of_head16 = of_head.astype(BF16)
    spread3 = jnp.concatenate([of_head] * 3, axis=0).astype(BF16)
    square_rows = lax.broadcasted_iota(jnp.int32, (q, q), 0)
    square_cols = lax.broadcasted_iota(jnp.int32, (q, q), 1)
    rate = jnp.zeros((heads, 1), F32)
    rate_row = lax.broadcasted_iota(jnp.int32, (heads, 1), 0)
    for h in range(heads):
        rate = jnp.where(rate_row == h, rate_ref[h], rate)

    def rows_of(c):
        return pl.ds(pl.multiple_of(c * q, q), q)

    def doc_row(c):
        return jnp.concatenate(
            [doc_ref[pl.ds(c * doc_rows + k, 1), :] for k in range(doc_rows)], axis=1
        ).astype(F32)

    def first_doc(c):
        return doc_ref[pl.ds(c * doc_rows, 1), 0:1].astype(F32)

    def last_doc(c):
        return doc_ref[pl.ds(c * doc_rows + doc_rows - 1, 1), lanes - 1:lanes].astype(F32)

    def to_lanes(column):
        return jnp.sum(of_head * column, axis=0, keepdims=True)

    def widen(value):
        parts = jnp.concatenate([p.astype(F32) for p in three_parts(value)], axis=0)
        return dot_tn(parts.astype(BF16), spread3)

    def stacked_dot(value, right):
        parts = jnp.concatenate([p.astype(F32) for p in three_parts(value)], axis=0)
        made = dot_nn(parts.astype(BF16), right)
        return made[:heads] + made[heads:2 * heads] + made[2 * heads:]

    state[0] = jnp.zeros((states, width), F32)
    back[chunks] = jnp.zeros((states, width), F32)

    def local_states(c, total):
        rows = rows_of(c)
        steps = step_ref[:, rows]
        upper = (square_rows <= square_cols).astype(F32).astype(BF16)
        decay = stacked_dot(-steps * rate, upper)
        whole = decay[:, q - 1:q]
        middle = 0.5 * whole
        g_scaled = g_ref[rows, :].astype(F32) * widen(jnp.exp(decay - middle))
        high, low = two_parts(g_scaled)
        ghi[rows, :], glo[rows, :] = high, low
        x_scale = widen(jnp.exp(middle - decay) * steps)
        scale[rows, :] = x_scale
        xh, xl = two_parts(x_ref[rows, :].astype(F32) * x_scale)
        xhi[rows, :], xlo[rows, :] = xh, xl
        docs = doc_row(c)
        column = jnp.transpose(jnp.broadcast_to(docs, (lanes, q)))
        doc_col[rows, :] = column
        half_row = to_lanes(jnp.exp(middle))
        half[pl.ds(c, 1), :] = half_row
        w_last = jnp.where(column == docs[:, q - 1:], w_ref[rows, :].astype(F32), 0.0).astype(BF16)
        r_first = jnp.where(column == docs[:, :1], r_ref[rows, :].astype(F32), 0.0).astype(BF16)
        made = (dot_tn(w_last, xh) + dot_tn(w_last, xl)) * half_row
        before = last_doc(jnp.maximum(c - 1, 0))
        kept = jnp.where(before == docs[:, q - 1:], half_row * half_row, 0.0)
        state[c + 1] = made + kept * state[c]
        back[c] = (dot_tn(r_first, high) + dot_tn(r_first, low)) * half_row
        phi_f[pl.ds(c, 1), :] = to_lanes(jnp.exp(total))
        return total + whole

    total = lax.fori_loop(0, chunks, local_states, jnp.zeros((heads, 1), F32))
    phi_f[pl.ds(chunks, 1), :] = to_lanes(jnp.exp(total))
    phi_b[pl.ds(chunks, 1), :] = jnp.ones((1, width), F32)

    @pl.loop(0, chunks)
    def _(i):
        c = chunks - 1 - i
        half_row = half[pl.ds(c, 1), :]
        square = half_row * half_row
        kept = jnp.where(first_doc(jnp.minimum(c + 1, chunks - 1)) == first_doc(c), square, 0.0)
        back[c] = back[c] + kept * back[c + 1]
        phi_b[pl.ds(c, 1), :] = phi_b[pl.ds(c + 1, 1), :] * square

    whole_row = to_lanes(total)
    first_here, last_here = first_doc(0), last_doc(chunks - 1)

    def put(ref, which, value, span, doc):
        ref[which, 0:states, :] = value
        ref[which, states:states + 1, :] = span
        ref[which, states + 1:states + 2, :] = jnp.broadcast_to(doc, (1, width))

    def span_of(ref, which):
        return ref[which, states:states + 1, :]

    def doc_of(ref, which):
        return ref[which, states + 1:states + 2, :]

    def value_of(ref, which):
        return ref[which, 0:states, :]

    def ctx_copies(which, step):
        made = []
        for side, send, recv, k in ((step, f_send, f_recv, 0), (n_ctx - step, b_send, b_recv, 1)):
            made.append(
                pltpu.make_async_remote_copy(
                    src_ref=send.at[which], dst_ref=recv.at[which],
                    send_sem=ctx_ss.at[which, k], recv_sem=ctx_rs.at[which, k],
                    device_id={"ctx": mod(me_ctx + side, n_ctx)},
                )
            )
        return made

    def intra(c):
        rows = rows_of(c)
        reads, writes = r_ref[rows, :], w_ref[rows, :]
        column = doc_col[rows, :]
        same = jnp.concatenate([column] * doc_rows, axis=1) == doc_row(c)
        lower = same & (square_rows >= square_cols)
        upper = same & (square_rows <= square_cols)
        xh, xl, gh, gl = xhi[rows, :], xlo[rows, :], ghi[rows, :], glo[rows, :]
        high, low = two_parts(jnp.where(lower, dot_nt(reads, writes), 0.0))
        out_acc[rows, :] = dot_nn(high, xh) + dot_nn(high, xl) + dot_nn(low, xh)
        high, low = two_parts(jnp.where(upper, dot_nt(writes, reads), 0.0))
        val_acc[rows, :] = dot_nn(high, gh) + dot_nn(high, gl) + dot_nn(low, gh)
        pairs = dot_nt(gh, xh) + dot_nt(gh, xl) + dot_nt(gl, xh)
        high, low = two_parts(jnp.where(lower, pairs, 0.0))
        to_read = dot_nn(high, writes) + dot_nn(low, writes)
        to_write = dot_tn(high, reads) + dot_tn(low, reads)
        for j in range(per):
            rw[c * per + j, 0] = to_write[j * block:(j + 1) * block]
            rw[c * per + j, 1] = to_read[j * block:(j + 1) * block]

    put(f_send, 0, state[chunks], whole_row, last_here)
    put(b_send, 0, back[0], whole_row, first_here)
    pl.semaphore_wait(barrier, n_head - 1 + 4)
    first_copies = ctx_copies(0, 1)
    for copy in first_copies:
        copy.start()
    cut = (0, (3 * chunks) // 8, (6 * chunks) // 8, chunks)
    pl.loop(cut[0], cut[1])(intra)
    for copy in first_copies:
        copy.wait()
    whole_decay = jnp.exp(whole_row)
    put(
        f_send, 1,
        value_of(f_send, 0) + jnp.where(doc_of(f_recv, 0) == last_here, whole_decay, 0.0) * value_of(f_recv, 0),
        whole_row + span_of(f_recv, 0), last_here,
    )
    put(
        b_send, 1,
        value_of(b_send, 0) + jnp.where(doc_of(b_recv, 0) == first_here, whole_decay, 0.0) * value_of(b_recv, 0),
        whole_row + span_of(b_recv, 0), first_here,
    )
    second_copies = ctx_copies(1, 2)
    for copy in second_copies:
        copy.start()
    pl.loop(cut[1], cut[2])(intra)
    for copy in second_copies:
        copy.wait()
    for send, recv, doc in ((f_send, f_recv, last_here), (b_send, b_recv, first_here)):
        joined = jnp.where(doc_of(recv, 1) == doc, jnp.exp(span_of(send, 1)), 0.0)
        put(send, 2, value_of(send, 1) + joined * value_of(recv, 1), whole_row, doc)
    third_copies = ctx_copies(2, 1)
    for copy in third_copies:
        copy.start()
    pl.loop(cut[2], cut[3])(intra)
    for copy in third_copies:
        copy.wait()

    doc_before, doc_after = doc_of(f_recv, 2)[:, :1], doc_of(b_recv, 2)[:, :1]

    def previous_doc(c):
        return jnp.where(c == 0, doc_before, last_doc(jnp.maximum(c - 1, 0)))

    def next_doc(c):
        return jnp.where(c == chunks - 1, doc_after, first_doc(jnp.minimum(c + 1, chunks - 1)))

    def state_at(k, doc):
        return state[k] + jnp.where(doc == doc_before, phi_f[pl.ds(k, 1), :], 0.0) * value_of(f_recv, 2)

    def back_at(k, doc):
        return back[k] + jnp.where(doc == doc_after, phi_b[pl.ds(k, 1), :], 0.0) * value_of(b_recv, 2)

    def rw_copy(b):
        o = mod(b - me, n_head)
        return pltpu.make_async_remote_copy(
            src_ref=rw.at[b], dst_ref=rw_in.at[o], send_sem=rw_ss.at[o], recv_sem=rw_rs.at[o],
            device_id={"head": b},
        )

    @pl.loop(0, chunks)
    def _(i):
        c = lax.rem(me // per + 1 + i, chunks)
        rows = rows_of(c)
        column = doc_col[rows, :]
        half_row = half[pl.ds(c, 1), :]
        before, after = previous_doc(c), next_doc(c)
        sh, sl = two_parts(state_at(c, before) * half_row)
        sphi[c], splo[c] = sh, sl
        bh, bl = two_parts(back_at(c + 1, after) * half_row)
        bphi[c], bplo[c] = bh, bl
        to_read = dot_nt(ghi[rows, :], sh) + dot_nt(ghi[rows, :], sl) + dot_nt(glo[rows, :], sh)
        to_write = dot_nt(xhi[rows, :], bh) + dot_nt(xhi[rows, :], bl) + dot_nt(xlo[rows, :], bh)
        to_read = jnp.where(column == before, to_read, 0.0)
        to_write = jnp.where(column == after, to_write, 0.0)
        for j in range(per):
            b = c * per + j
            rw[b, 0] += to_write[j * block:(j + 1) * block]
            rw[b, 1] += to_read[j * block:(j + 1) * block]

            @pl.when(b != me)
            def _():
                rw_copy(b).start()

    @pl.loop(0, chunks)
    def _(c):
        rows = rows_of(c)
        column = doc_col[rows, :]
        docs = doc_row(c)
        before, after, last = previous_doc(c), next_doc(c), docs[:, q - 1:]
        reads = jnp.where(column == before, r_ref[rows, :].astype(F32), 0.0).astype(BF16)
        writes = jnp.where(column == after, w_ref[rows, :].astype(F32), 0.0).astype(BF16)
        out = out_acc[rows, :] + dot_nn(reads, sphi[c]) + dot_nn(reads, splo[c])
        val = val_acc[rows, :] + dot_nn(writes, bphi[c]) + dot_nn(writes, bplo[c])
        vg_ref[rows, :] = (scale[rows, :] * val).astype(BF16)
        g_scaled = ghi[rows, :].astype(F32) + glo[rows, :].astype(F32)
        x_scaled = xhi[rows, :].astype(F32) + xlo[rows, :].astype(F32)
        high, low = two_parts(x_scaled * val)
        at_write = dot_nt(of_head16, high) + dot_nt(of_head16, low)
        high, low = two_parts(g_scaled * out)
        at_read = dot_nt(of_head16, high) + dot_nt(of_head16, low)
        lower = (jnp.concatenate([column] * doc_rows, axis=1) == docs) & (square_rows >= square_cols)
        later = stacked_dot(at_read - at_write, lower.astype(F32).astype(BF16))
        crossing = jnp.sum(state_at(c + 1, last) * back_at(c + 1, after), axis=0, keepdims=True)
        crossing = jnp.sum(of_head * crossing, axis=1, keepdims=True)
        crossing = jnp.where(last == after, crossing, 0.0)
        later = later + jnp.where(docs == last, crossing, 0.0)
        sg_ref[:, rows] = at_write / step_ref[:, rows] - rate * later

    @pl.loop(1, n_head)
    def _(o):
        rw_copy(mod(me + o, n_head)).wait_recv()

    def gathered(k):
        return lax.fori_loop(1, n_head, lambda o, held: held + rw_in[o, k], rw[me, k])

    wg_ref[...] = gathered(0)
    rg_ref[...] = gathered(1)

    @pl.loop(1, n_head)
    def _(o):
        rw_copy(mod(me + o, n_head)).wait_send()


def shards(mesh_shape, values, step_sizes, decay_rates, write_keys, read_keys, doc_ids, out_grad):
    n_ctx, n_head = mesh_shape
    length, width = values.shape
    heads = decay_rates.shape[0]
    states = write_keys.shape[1]
    chunks = length // QCHUNK
    block = length // n_head
    vmem = pl.BlockSpec(memory_space=pltpu.VMEM)
    wide16 = pltpu.VMEM((length, width), BF16)
    wide32 = pltpu.VMEM((length, width), F32)
    message = pltpu.VMEM((ROUNDS, states + 8, width), F32)
    value_grad, step_grad, write_grad, read_grad = pl.pallas_call(
        partial(kernel, n_ctx, n_head),
        out_shape=(
            jax.ShapeDtypeStruct((length, width), BF16),
            jax.ShapeDtypeStruct((heads, length), F32),
            jax.ShapeDtypeStruct((block, states), F32),
            jax.ShapeDtypeStruct((block, states), F32),
        ),
        in_specs=[vmem, vmem, vmem, pl.BlockSpec(memory_space=pltpu.SMEM), vmem, vmem, vmem],
        out_specs=(vmem, vmem, vmem, vmem),
        scratch_shapes=[
            wide16, wide16, wide16, wide16, wide32, wide32, wide32,
            pltpu.VMEM((length, 128), F32),
            pltpu.VMEM((n_head, 2, block, states), F32),
            pltpu.VMEM((n_head, 2, block, states), F32),
            pltpu.VMEM((chunks + 1, states, width), F32),
            pltpu.VMEM((chunks + 1, states, width), F32),
            pltpu.VMEM((chunks, width), F32),
            pltpu.VMEM((chunks + 1, width), F32),
            pltpu.VMEM((chunks + 1, width), F32),
            pltpu.VMEM((chunks, states, width), BF16),
            pltpu.VMEM((chunks, states, width), BF16),
            pltpu.VMEM((chunks, states, width), BF16),
            pltpu.VMEM((chunks, states, width), BF16),
            message, message, message, message,
            pltpu.SemaphoreType.DMA((ROUNDS, 2)),
            pltpu.SemaphoreType.DMA((ROUNDS, 2)),
            pltpu.SemaphoreType.DMA((n_head,)),
            pltpu.SemaphoreType.DMA((n_head,)),
        ],
        compiler_params=pltpu.CompilerParams(
            collective_id=0, has_side_effects=True, vmem_limit_bytes=60 * 2**20
        ),
    )(
        values, out_grad, step_sizes.T, decay_rates, write_keys, read_keys,
        doc_ids.reshape(length // 128, 128),
    )
    return value_grad, step_grad.T, write_grad, read_grad


def solution(mesh):
    return jax.shard_map(
        partial(shards, (mesh.shape["ctx"], mesh.shape["head"])),
        mesh=mesh,
        in_specs=(
            P("ctx", "head"),
            P("ctx", "head"),
            P("head"),
            P("ctx", None),
            P("ctx", None),
            P("ctx"),
            P("ctx", "head"),
        ),
        out_specs=(
            P("ctx", "head"),
            P("ctx", "head"),
            P(("ctx", "head"), None),
            P(("ctx", "head"), None),
        ),
        check_vma=False,
    )
```

time: 641 us -> 80.1 us (0.12)
  the two profiles are of different devices: /device:TPU:0 before, /device:TPU:57 now
where the time goes in v1:
time: 80.1 us; the launch traced here: 80 us
  Pallas kernels  74.3 us (93%)
  local copies, waits for them, and re-layouts  4.99 us (6%)
    pallas_call x1, Pallas kernels, shards(): pl.pallas_call(partial(kernel, n_ctx, n_head), out_shape=(jax.ShapeDtypeS...  74.3 us
    unnamed x10, local copies, waits for them, and re-layouts  4.99 us

profile of v1, /device:TPU:57, one launch (start us, length us, event | category | flops | bytes accessed | tf_op | source)
XLA Modules:
  0.0 80.0 jit_solution(16576060513297162907)
XLA Ops:
  0.6 74.3 %shard_map.102 = (bf16[2048,512]{1,0:T(8,128)(2,1)}, f32[8,2048]{1,0:T(8,128)}, f32[128,128]{1,0:T(8,128)}, f32[128,128]{1,0:T(8,128)}) custom-call(bf16[2048,512]{1,0:T(8,128)(2,1)} %x_ref.1, bf16[2048,512]{1,0:T(8,128)(2,1)} %g_ref.1, f32[8,2048]{1,0:T(8,128)} %bitcast.3, f32[8]{0:T(128)} %rate_ref.1, bf16[2048,128]{1,0:T(8,128)(2,1)} %w_ref.1, ...), custom_call_target="tpu_custom_call" | custom-call | tf_op jit(solution)/shard_map/pallas_call | solution.py:341
  75.0 0.0 copy-start.2
  75.0 0.0 copy-start.1
  75.0 0.0 copy-start
  75.0 3.1 %copy.15 = bf16[2048,512]{1,0:T(8,128)(2,1)} copy(bf16[2048,512]{1,0:T(8,128)(2,1)} %get-tuple-element.16) | data formatting | bytes 4194304
  78.1 0.0 copy-done.2
  78.1 0.6 copy.16
  78.7 0.0 copy-done.1
  78.7 0.6 copy.17
  79.4 0.0 copy-done
  79.4 0.6 copy.18
Async XLA Ops:
  75.0 3.1 %copy-start.2 = (f32[8,2048]{1,0:T(8,128)S(1)}, f32[8,2048]{1,0:T(8,128)}, u32[]{:S(2)}) copy-start(f32[8,2048]{1,0:T(8,128)} %get-tuple-element.9) | copy-start | bytes 196612
  75.0 3.7 %copy-start.1 = (f32[128,128]{1,0:T(8,128)S(1)}, f32[128,128]{1,0:T(8,128)}, u32[]{:S(2)}) copy-start(f32[128,128]{1,0:T(8,128)} %get-tuple-element.18) | copy-start | bytes 196612
  75.0 4.4 %copy-start = (f32[128,128]{1,0:T(8,128)S(1)}, f32[128,128]{1,0:T(8,128)}, u32[]{:S(2)}) copy-start(f32[128,128]{1,0:T(8,128)} %get-tuple-element.19) | copy-start | bytes 196612

commit v2 on v1

--- a/solution.py
+++ b/solution.py
@@ -1,3 +1,4 @@
+import math
 from functools import partial
 
 import jax
@@ -8,7 +9,6 @@
 from jax.sharding import PartitionSpec as P
 
 QCHUNK = 256
-ROUNDS = 3
 F32 = jnp.float32
 BF16 = jnp.bfloat16
 
@@ -48,9 +48,12 @@
 def kernel(
     n_ctx, n_head, x_ref, g_ref, step_ref, rate_ref, w_ref, r_ref, doc_ref,
     vg_ref, sg_ref, wg_ref, rg_ref,
-    xhi, xlo, ghi, glo, scale, out_acc, val_acc, doc_col, rw, rw_in,
+    xhi, xlo, ghi, glo, scale, out_acc, val_acc, doc_col,
+    r_acc, w_acc, r_in, w_in, r_in2, w_in2,
     state, back, half, phi_f, phi_b, sphi, splo, bphi, bplo,
-    f_send, f_recv, b_send, b_recv, ctx_ss, ctx_rs, rw_ss, rw_rs,
+    e_out, b_out, e_sib, b_sib, f_out, k_out, f_in, k_in, s_out, g_out, s_in, g_in,
+    sib_ss, sib_rs, z_ss, z_rs, last_ss, last_rs,
+    r_ss, r_rs, w_ss, w_rs, r2_ss, r2_rs, w2_ss, w2_rs,
 ):
     length, width = x_ref.shape
     heads = step_ref.shape[0]
@@ -58,20 +61,41 @@
     states = w_ref.shape[1]
     q = QCHUNK
     chunks = length // q
+    side = math.isqrt(n_head)
+    n_z = n_ctx // 2
+    group = length // side
     block = length // n_head
-    per = q // block
     lanes = 128
     doc_rows = q // lanes
+    hw = width // 2
     me_ctx, me = lax.axis_index("ctx"), lax.axis_index("head")
+    me_z, core = me_ctx // 2, lax.rem(me_ctx, 2)
+    me_x, me_y = me // side, lax.rem(me, side)
+
+    def at_z(z):
+        return {"ctx": z * 2 + core}
+
+    def at_xy(x, y):
+        return {"head": x * side + y}
+
+    sibling = {"ctx": me_ctx + 1 - 2 * core}
+
+    def put(ref, which, value, span, doc):
+        ref[which, 0:states, :] = value
+        ref[which, states:states + 1, :] = span
+        ref[which, states + 1:states + 2, :] = jnp.broadcast_to(doc, (1, hw))
+
+    for far in range(2):
+        for ref in (f_in, k_in):
+            put(ref, far, jnp.zeros((states, hw), F32), jnp.zeros((1, hw), F32), jnp.full((1, 1), -1.0, F32))
 
     barrier = pltpu.get_barrier_semaphore()
-    for step in (1, 2):
-        for side in (step, n_ctx - step):
-            pl.semaphore_signal(barrier, inc=1, device_id={"ctx": mod(me_ctx + side, n_ctx)})
-
-    @pl.loop(1, n_head)
-    def _(o):
-        pl.semaphore_signal(barrier, inc=1, device_id={"head": mod(me + o, n_head)})
+    pl.semaphore_signal(barrier, inc=1, device_id=sibling)
+    for o in range(1, n_z):
+        pl.semaphore_signal(barrier, inc=1, device_id=at_z(mod(me_z + o, n_z)))
+    for o in range(1, side):
+        pl.semaphore_signal(barrier, inc=1, device_id=at_xy(mod(me_x + o, side), me_y))
+        pl.semaphore_signal(barrier, inc=1, device_id=at_xy(me_x, mod(me_y + o, side)))
 
     head_rows = lax.broadcasted_iota(jnp.int32, (heads, width), 0)
     head_lanes = lax.broadcasted_iota(jnp.int32, (heads, width), 1)
@@ -159,11 +183,6 @@
     whole_row = to_lanes(total)
     first_here, last_here = first_doc(0), last_doc(chunks - 1)
 
-    def put(ref, which, value, span, doc):
-        ref[which, 0:states, :] = value
-        ref[which, states:states + 1, :] = span
-        ref[which, states + 1:states + 2, :] = jnp.broadcast_to(doc, (1, width))
-
     def span_of(ref, which):
         return ref[which, states:states + 1, :]
 
@@ -173,17 +192,20 @@
     def value_of(ref, which):
         return ref[which, 0:states, :]
 
-    def ctx_copies(which, step):
-        made = []
-        for side, send, recv, k in ((step, f_send, f_recv, 0), (n_ctx - step, b_send, b_recv, 1)):
-            made.append(
-                pltpu.make_async_remote_copy(
-                    src_ref=send.at[which], dst_ref=recv.at[which],
-                    send_sem=ctx_ss.at[which, k], recv_sem=ctx_rs.at[which, k],
-                    device_id={"ctx": mod(me_ctx + side, n_ctx)},
-                )
-            )
-        return made
+    def joined(near, near_doc, near_span, far, far_doc):
+        return near + jnp.where(near_doc == far_doc, jnp.exp(near_span), 0.0) * far
+
+    def sib_copy(k, src, dst, ss, rs):
+        return pltpu.make_async_remote_copy(
+            src_ref=src, dst_ref=dst, send_sem=ss.at[k], recv_sem=rs.at[k], device_id=sibling
+        )
+
+    def z_copy(k, far):
+        src, dst, to = (f_out, f_in, me_z + far) if k == 0 else (k_out, k_in, me_z - far)
+        return pltpu.make_async_remote_copy(
+            src_ref=src.at[0], dst_ref=dst.at[far - 1], send_sem=z_ss.at[k, far - 1],
+            recv_sem=z_rs.at[k, far - 1], device_id=at_z(to),
+        )
 
     def intra(c):
         rows = rows_of(c)
@@ -201,48 +223,83 @@
         high, low = two_parts(jnp.where(lower, pairs, 0.0))
         to_read = dot_nn(high, writes) + dot_nn(low, writes)
         to_write = dot_tn(high, reads) + dot_tn(low, reads)
-        for j in range(per):
-            rw[c * per + j, 0] = to_write[j * block:(j + 1) * block]
-            rw[c * per + j, 1] = to_read[j * block:(j + 1) * block]
-
-    put(f_send, 0, state[chunks], whole_row, last_here)
-    put(b_send, 0, back[0], whole_row, first_here)
-    pl.semaphore_wait(barrier, n_head - 1 + 4)
-    first_copies = ctx_copies(0, 1)
-    for copy in first_copies:
+        r_acc[rows, :] = to_read
+        w_acc[rows, :] = to_write
+
+    for k in range(2):
+        lane = slice(k * hw, (k + 1) * hw)
+        put(e_out, k, state[chunks][:, lane], whole_row[:, lane], last_here)
+        put(b_out, k, back[0][:, lane], whole_row[:, lane], first_here)
+    pl.semaphore_wait(barrier, 1 + n_z - 1 + 2 * (side - 1))
+    sib_copies = (
+        sib_copy(0, e_out.at[1 - core], e_sib.at[0], sib_ss, sib_rs),
+        sib_copy(1, b_out.at[1 - core], b_sib.at[0], sib_ss, sib_rs),
+    )
+    for copy in sib_copies:
         copy.start()
-    cut = (0, (3 * chunks) // 8, (6 * chunks) // 8, chunks)
-    pl.loop(cut[0], cut[1])(intra)
-    for copy in first_copies:
+    cuts = (0, chunks // 8, (7 * chunks) // 8, chunks)
+    pl.loop(cuts[0], cuts[1])(intra)
+    for copy in sib_copies:
         copy.wait()
-    whole_decay = jnp.exp(whole_row)
-    put(
-        f_send, 1,
-        value_of(f_send, 0) + jnp.where(doc_of(f_recv, 0) == last_here, whole_decay, 0.0) * value_of(f_recv, 0),
-        whole_row + span_of(f_recv, 0), last_here,
+    low, mine, other = core == 0, core, 0
+    e_low = jnp.where(low, value_of(e_out, mine), value_of(e_sib, other))
+    e_high = jnp.where(low, value_of(e_sib, other), value_of(e_out, mine))
+    b_low = jnp.where(low, value_of(b_out, mine), value_of(b_sib, other))
+    b_high = jnp.where(low, value_of(b_sib, other), value_of(b_out, mine))
+    span_low = jnp.where(low, span_of(e_out, mine), span_of(e_sib, other))
+    span_high = jnp.where(low, span_of(e_sib, other), span_of(e_out, mine))
+    last_low = jnp.where(low, doc_of(e_out, mine), doc_of(e_sib, other))
+    last_high = jnp.where(low, doc_of(e_sib, other), doc_of(e_out, mine))
+    first_low = jnp.where(low, doc_of(b_out, mine), doc_of(b_sib, other))
+    first_high = jnp.where(low, doc_of(b_sib, other), doc_of(b_out, mine))
+    put(f_out, 0, joined(e_high, last_high, span_high, e_low, last_low), span_low + span_high, last_high)
+    put(k_out, 0, joined(b_low, first_low, span_low, b_high, first_high), span_low + span_high, first_low)
+    for far in (1, 2):
+        if far < n_z:
+
+            @pl.when(me_z + far < n_z)
+            def _():
+                z_copy(0, far).start()
+
+            @pl.when(me_z - far >= 0)
+            def _():
+                z_copy(1, far).start()
+
+    pl.loop(cuts[1], cuts[2], unroll=2)(intra)
+    for far in (1, 2):
+        if far < n_z:
+
+            @pl.when(me_z - far >= 0)
+            def _():
+                z_copy(0, far).wait_recv()
+
+            @pl.when(me_z + far < n_z)
+            def _():
+                z_copy(1, far).wait_recv()
+
+    s_chip = joined(value_of(f_in, 0), doc_of(f_in, 0), span_of(f_in, 0), value_of(f_in, 1), doc_of(f_in, 1))
+    g_chip = joined(value_of(k_in, 0), doc_of(k_in, 0), span_of(k_in, 0), value_of(k_in, 1), doc_of(k_in, 1))
+    s_high = joined(value_of(e_out, mine), last_low, span_low, s_chip, doc_of(f_in, 0))
+    s_high = jnp.where(low, s_high, joined(value_of(e_sib, other), last_low, span_low, s_chip, doc_of(f_in, 0)))
+    g_low = joined(value_of(b_sib, other), first_high, span_high, g_chip, doc_of(k_in, 0))
+    g_low = jnp.where(low, g_low, joined(value_of(b_out, mine), first_high, span_high, g_chip, doc_of(k_in, 0)))
+    s_doc_low, s_doc_high = doc_of(f_in, 0), last_low
+    g_doc_low, g_doc_high = first_high, doc_of(k_in, 0)
+    put(s_out, 0, jnp.where(low, s_high, s_chip), span_low, jnp.where(low, s_doc_high, s_doc_low))
+    put(g_out, 0, jnp.where(low, g_chip, g_low), span_low, jnp.where(low, g_doc_high, g_doc_low))
+    last_copies = (
+        sib_copy(0, s_out.at[0], s_in.at[mine], last_ss, last_rs),
+        sib_copy(1, g_out.at[0], g_in.at[mine], last_ss, last_rs),
     )
-    put(
-        b_send, 1,
-        value_of(b_send, 0) + jnp.where(doc_of(b_recv, 0) == first_here, whole_decay, 0.0) * value_of(b_recv, 0),
-        whole_row + span_of(b_recv, 0), first_here,
-    )
-    second_copies = ctx_copies(1, 2)
-    for copy in second_copies:
+    for copy in last_copies:
         copy.start()
-    pl.loop(cut[1], cut[2])(intra)
-    for copy in second_copies:
+    put(s_in, mine, jnp.where(low, s_chip, s_high), span_low, jnp.where(low, s_doc_low, s_doc_high))
+    put(g_in, mine, jnp.where(low, g_low, g_chip), span_low, jnp.where(low, g_doc_low, g_doc_high))
+    pl.loop(cuts[2], cuts[3])(intra)
+    for copy in last_copies:
         copy.wait()
-    for send, recv, doc in ((f_send, f_recv, last_here), (b_send, b_recv, first_here)):
-        joined = jnp.where(doc_of(recv, 1) == doc, jnp.exp(span_of(send, 1)), 0.0)
-        put(send, 2, value_of(send, 1) + joined * value_of(recv, 1), whole_row, doc)
-    third_copies = ctx_copies(2, 1)
-    for copy in third_copies:
-        copy.start()
-    pl.loop(cut[2], cut[3])(intra)
-    for copy in third_copies:
-        copy.wait()
-
-    doc_before, doc_after = doc_of(f_recv, 2)[:, :1], doc_of(b_recv, 2)[:, :1]
+
+    doc_before, doc_after = doc_of(s_in, 0)[:, :1], doc_of(g_in, 0)[:, :1]
 
     def previous_doc(c):
         return jnp.where(c == 0, doc_before, last_doc(jnp.maximum(c - 1, 0)))
@@ -251,21 +308,45 @@
         return jnp.where(c == chunks - 1, doc_after, first_doc(jnp.minimum(c + 1, chunks - 1)))
 
     def state_at(k, doc):
-        return state[k] + jnp.where(doc == doc_before, phi_f[pl.ds(k, 1), :], 0.0) * value_of(f_recv, 2)
+        entered = jnp.concatenate([value_of(s_in, 0), value_of(s_in, 1)], axis=1)
+        return state[k] + jnp.where(doc == doc_before, phi_f[pl.ds(k, 1), :], 0.0) * entered
 
     def back_at(k, doc):
-        return back[k] + jnp.where(doc == doc_after, phi_b[pl.ds(k, 1), :], 0.0) * value_of(b_recv, 2)
-
-    def rw_copy(b):
-        o = mod(b - me, n_head)
+        entered = jnp.concatenate([value_of(g_in, 0), value_of(g_in, 1)], axis=1)
+        return back[k] + jnp.where(doc == doc_after, phi_b[pl.ds(k, 1), :], 0.0) * entered
+
+    def span_rows(start, count):
+        return pl.ds(pl.multiple_of(start, count), count)
+
+    def r_copy(o):
+        x = mod(me_x + o, side)
         return pltpu.make_async_remote_copy(
-            src_ref=rw.at[b], dst_ref=rw_in.at[o], send_sem=rw_ss.at[o], recv_sem=rw_rs.at[o],
-            device_id={"head": b},
+            src_ref=r_acc.at[span_rows(x * group, group)], dst_ref=r_in.at[o - 1],
+            send_sem=r_ss.at[o - 1], recv_sem=r_rs.at[o - 1], device_id=at_xy(x, me_y),
         )
 
-    @pl.loop(0, chunks)
-    def _(i):
-        c = lax.rem(me // per + 1 + i, chunks)
+    def w_copy(o, x):
+        y = mod(me_y + o, side)
+        return pltpu.make_async_remote_copy(
+            src_ref=w_acc.at[span_rows((x * side + y) * block, block)], dst_ref=w_in.at[o - 1, x],
+            send_sem=w_ss.at[o - 1, x], recv_sem=w_rs.at[o - 1, x], device_id=at_xy(me_x, y),
+        )
+
+    def r_copy2(o):
+        y = mod(me_y + o, side)
+        return pltpu.make_async_remote_copy(
+            src_ref=r_acc.at[span_rows((me_x * side + y) * block, block)], dst_ref=r_in2.at[o - 1],
+            send_sem=r2_ss.at[o - 1], recv_sem=r2_rs.at[o - 1], device_id=at_xy(me_x, y),
+        )
+
+    def w_copy2(o):
+        x = mod(me_x + o, side)
+        return pltpu.make_async_remote_copy(
+            src_ref=w_acc.at[span_rows((x * side + me_y) * block, block)], dst_ref=w_in2.at[o - 1],
+            send_sem=w2_ss.at[o - 1], recv_sem=w2_rs.at[o - 1], device_id=at_xy(x, me_y),
+        )
+
+    def key_grads(c):
         rows = rows_of(c)
         column = doc_col[rows, :]
         half_row = half[pl.ds(c, 1), :]
@@ -278,17 +359,22 @@
         to_write = dot_nt(xhi[rows, :], bh) + dot_nt(xhi[rows, :], bl) + dot_nt(xlo[rows, :], bh)
         to_read = jnp.where(column == before, to_read, 0.0)
         to_write = jnp.where(column == after, to_write, 0.0)
-        for j in range(per):
-            b = c * per + j
-            rw[b, 0] += to_write[j * block:(j + 1) * block]
-            rw[b, 1] += to_read[j * block:(j + 1) * block]
-
-            @pl.when(b != me)
-            def _():
-                rw_copy(b).start()
-
-    @pl.loop(0, chunks)
-    def _(c):
+        r_acc[rows, :] += to_read
+        w_acc[rows, :] += to_write
+
+    @pl.loop(0, side)
+    def _(i):
+        x = mod(me_x + 1 + i, side)
+        pl.loop(0, chunks // side, unroll=True)(lambda k: key_grads(x * (chunks // side) + k))
+
+        @pl.when(i < side - 1)
+        def _():
+            r_copy(i + 1).start()
+
+        for o in range(1, side):
+            w_copy(o, x).start()
+
+    def rest(c):
         rows = rows_of(c)
         column = doc_col[rows, :]
         docs = doc_row(c)
@@ -312,19 +398,61 @@
         later = later + jnp.where(docs == last, crossing, 0.0)
         sg_ref[:, rows] = at_write / step_ref[:, rows] - rate * later
 
-    @pl.loop(1, n_head)
-    def _(o):
-        rw_copy(mod(me + o, n_head)).wait_recv()
-
-    def gathered(k):
-        return lax.fori_loop(1, n_head, lambda o, held: held + rw_in[o, k], rw[me, k])
-
-    wg_ref[...] = gathered(0)
-    rg_ref[...] = gathered(1)
-
-    @pl.loop(1, n_head)
-    def _(o):
-        rw_copy(mod(me + o, n_head)).wait_send()
+    later_from = (5 * chunks) // 8
+    pl.loop(0, later_from)(rest)
+    for o in range(1, side):
+        r_copy(o).wait_recv()
+
+        @pl.loop(0, side)
+        def _(x):
+            w_copy(o, x).wait_recv()
+
+    for o in range(side):
+        y = mod(me_y + o, side)
+        rows = span_rows((me_x * side + y) * block, block)
+        held = r_acc[rows, :]
+        for k in range(side - 1):
+            held = held + r_in[k, span_rows(y * block, block), :]
+        r_acc[rows, :] = held
+        if o > 0:
+            r_copy2(o).start()
+        x = mod(me_x + o, side)
+        rows = span_rows((x * side + me_y) * block, block)
+        held = w_acc[rows, :]
+        for k in range(side - 1):
+            held = held + w_in[k, x]
+        w_acc[rows, :] = held
+        if o > 0:
+            w_copy2(o).start()
+    pl.loop(later_from, chunks)(rest)
+    mine_rows = span_rows(me * block, block)
+    read_total, write_total = r_acc[mine_rows, :], w_acc[mine_rows, :]
+    for o in range(1, side):
+        r_copy2(o).wait_recv()
+        read_total = read_total + r_in2[o - 1]
+        w_copy2(o).wait_recv()
+        write_total = write_total + w_in2[o - 1]
+    wg_ref[...] = write_total
+    rg_ref[...] = read_total
+    for far in (1, 2):
+        if far < n_z:
+
+            @pl.when(me_z + far < n_z)
+            def _():
+                z_copy(0, far).wait_send()
+
+            @pl.when(me_z - far >= 0)
+            def _():
+                z_copy(1, far).wait_send()
+
+    for o in range(1, side):
+        r_copy(o).wait_send()
+        r_copy2(o).wait_send()
+        w_copy2(o).wait_send()
+
+        @pl.loop(0, side)
+        def _(x):
+            w_copy(o, x).wait_send()
 
 
 def shards(mesh_shape, values, step_sizes, decay_rates, write_keys, read_keys, doc_ids, out_grad):
@@ -334,10 +462,17 @@
     states = write_keys.shape[1]
     chunks = length // QCHUNK
     block = length // n_head
+    side = math.isqrt(n_head)
     vmem = pl.BlockSpec(memory_space=pltpu.VMEM)
     wide16 = pltpu.VMEM((length, width), BF16)
     wide32 = pltpu.VMEM((length, width), F32)
-    message = pltpu.VMEM((ROUNDS, states + 8, width), F32)
+    def messages(count):
+        return pltpu.VMEM((count, states + 8, width // 2), F32)
+
+    def semaphores(*shape):
+        return [pltpu.SemaphoreType.DMA(shape)] * 2
+
+    others = max(side - 1, 1)
     value_grad, step_grad, write_grad, read_grad = pl.pallas_call(
         partial(kernel, n_ctx, n_head),
         out_shape=(
@@ -351,8 +486,12 @@
         scratch_shapes=[
             wide16, wide16, wide16, wide16, wide32, wide32, wide32,
             pltpu.VMEM((length, 128), F32),
-            pltpu.VMEM((n_head, 2, block, states), F32),
-            pltpu.VMEM((n_head, 2, block, states), F32),
+            pltpu.VMEM((length, states), F32),
+            pltpu.VMEM((length, states), F32),
+            pltpu.VMEM((others, length // side, states), F32),
+            pltpu.VMEM((others, side, block, states), F32),
+            pltpu.VMEM((others, block, states), F32),
+            pltpu.VMEM((others, block, states), F32),
             pltpu.VMEM((chunks + 1, states, width), F32),
             pltpu.VMEM((chunks + 1, states, width), F32),
             pltpu.VMEM((chunks, width), F32),
@@ -362,11 +501,10 @@
             pltpu.VMEM((chunks, states, width), BF16),
             pltpu.VMEM((chunks, states, width), BF16),
             pltpu.VMEM((chunks, states, width), BF16),
-            message, message, message, message,
-            pltpu.SemaphoreType.DMA((ROUNDS, 2)),
-            pltpu.SemaphoreType.DMA((ROUNDS, 2)),
-            pltpu.SemaphoreType.DMA((n_head,)),
-            pltpu.SemaphoreType.DMA((n_head,)),
+            messages(2), messages(2), messages(1), messages(1), messages(1), messages(1),
+            messages(2), messages(2), messages(1), messages(1), messages(2), messages(2),
+            *semaphores(2), *semaphores(2, 2), *semaphores(2),
+            *semaphores(others), *semaphores(others, side), *semaphores(others), *semaphores(others),
         ],
         compiler_params=pltpu.CompilerParams(
             collective_id=0, has_side_effects=True, vmem_limit_bytes=60 * 2**20

time: 80.1 us -> 56.1 us (0.70)
  the two profiles are of different devices: /device:TPU:57 before, /device:TPU:0 now
where the time goes in v2:
time: 56.1 us; the launch traced here: 55.2 us
  Pallas kernels  49.5 us (88%)
  local copies, waits for them, and re-layouts  4.99 us (9%)
  between operations  0.67 us (1%)
    pallas_call x1, Pallas kernels, shards(): pl.pallas_call(partial(kernel, n_ctx, n_head), out_shape=(jax.ShapeDtypeS...  49.5 us
    unnamed x10, local copies, waits for them, and re-layouts  4.99 us

profile of v2, /device:TPU:0, one launch (start us, length us, event | category | flops | bytes accessed | tf_op | source)
XLA Modules:
  0.0 55.2 jit_solution(15821418963470607686)
XLA Ops:
  0.6 49.5 %shard_map.102 = (bf16[2048,512]{1,0:T(8,128)(2,1)}, f32[8,2048]{1,0:T(8,128)}, f32[128,128]{1,0:T(8,128)}, f32[128,128]{1,0:T(8,128)}) custom-call(bf16[2048,512]{1,0:T(8,128)(2,1)} %x_ref.1, bf16[2048,512]{1,0:T(8,128)(2,1)} %g_ref.1, f32[8,2048]{1,0:T(8,128)} %bitcast.3, f32[8]{0:T(128)} %rate_ref.1, bf16[2048,128]{1,0:T(8,128)(2,1)} %w_ref.1, ...), custom_call_target="tpu_custom_call" | custom-call | tf_op jit(solution)/shard_map/pallas_call | solution.py:476
  50.2 0.0 copy-start.2
  50.2 0.0 copy-start.1
  50.2 0.0 copy-start
  50.2 3.1 %copy.15 = bf16[2048,512]{1,0:T(8,128)(2,1)} copy(bf16[2048,512]{1,0:T(8,128)(2,1)} %get-tuple-element.16) | data formatting | bytes 4194304
  53.3 0.0 copy-done.2
  53.3 0.6 %copy.16 = f32[2048,8]{0,1:T(8,128)} copy(f32[2048,8]{0,1:T(8,128)S(1)} %bitcast.4) | data formatting | bytes 131072
  53.9 0.0 copy-done.1
  53.9 0.6 %copy.17 = f32[128,128]{1,0:T(8,128)} copy(f32[128,128]{1,0:T(8,128)S(1)} %copy-done.1) | data formatting | bytes 131072
  54.5 0.0 copy-done
  54.5 0.6 %copy.18 = f32[128,128]{1,0:T(8,128)} copy(f32[128,128]{1,0:T(8,128)S(1)} %copy-done) | data formatting | bytes 131072
Async XLA Ops:
  50.2 3.1 %copy-start.2 = (f32[8,2048]{1,0:T(8,128)S(1)}, f32[8,2048]{1,0:T(8,128)}, u32[]{:S(2)}) copy-start(f32[8,2048]{1,0:T(8,128)} %get-tuple-element.9) | copy-start | bytes 196612
  50.2 3.7 %copy-start.1 = (f32[128,128]{1,0:T(8,128)S(1)}, f32[128,128]{1,0:T(8,128)}, u32[]{:S(2)}) copy-start(f32[128,128]{1,0:T(8,128)} %get-tuple-element.18) | copy-start | bytes 196612
  50.2 4.4 %copy-start = (f32[128,128]{1,0:T(8,128)S(1)}, f32[128,128]{1,0:T(8,128)}, u32[]{:S(2)}) copy-start(f32[128,128]{1,0:T(8,128)} %get-tuple-element.19) | copy-start | bytes 196612

commit v3 on v2

--- a/solution.py
+++ b/solution.py
@@ -46,19 +46,20 @@
 
 
 def kernel(
-    n_ctx, n_head, x_ref, g_ref, step_ref, rate_ref, w_ref, r_ref, doc_ref,
+    n_ctx, n_head, x_hbm, g_hbm, step_ref, rate_ref, w_hbm, r_hbm, doc_ref,
     vg_ref, sg_ref, wg_ref, rg_ref,
+    x_ref, g_ref, w_ref, r_ref, in_sems, u_parts, v_parts, grows, shrinks, entry,
     xhi, xlo, ghi, glo, scale, out_acc, val_acc, doc_col,
-    r_acc, w_acc, r_in, w_in, r_in2, w_in2,
+    r_acc, w_acc, r_mid, w_mid, r_in, w_in, r_in2, w_in2,
     state, back, half, phi_f, phi_b, sphi, splo, bphi, bplo,
     e_out, b_out, e_sib, b_sib, f_out, k_out, f_in, k_in, s_out, g_out, s_in, g_in,
     sib_ss, sib_rs, z_ss, z_rs, last_ss, last_rs,
-    r_ss, r_rs, w_ss, w_rs, r2_ss, r2_rs, w2_ss, w2_rs,
+    ra_ss, ra_rs, wa_ss, wa_rs, r_ss, r_rs, w_ss, w_rs, r2_ss, r2_rs, w2_ss, w2_rs,
 ):
-    length, width = x_ref.shape
+    length, width = x_hbm.shape
     heads = step_ref.shape[0]
     head_size = width // heads
-    states = w_ref.shape[1]
+    states = w_hbm.shape[1]
     q = QCHUNK
     chunks = length // q
     side = math.isqrt(n_head)
@@ -85,6 +86,19 @@
         ref[which, states:states + 1, :] = span
         ref[which, states + 1:states + 2, :] = jnp.broadcast_to(doc, (1, hw))
 
+    def arrivals(c):
+        rows = pl.ds(pl.multiple_of(c * q, q), q)
+        pairs = ((g_hbm, g_ref), (x_hbm, x_ref), (w_hbm, w_ref), (r_hbm, r_ref))
+        return [
+            pltpu.make_async_copy(src.at[rows], dst.at[rows], in_sems.at[k, c])
+            for k, (src, dst) in enumerate(pairs)
+        ]
+
+    @pl.loop(0, chunks)
+    def _(c):
+        for copy in arrivals(c):
+            copy.start()
+
     for far in range(2):
         for ref in (f_in, k_in):
             put(ref, far, jnp.zeros((states, hw), F32), jnp.zeros((1, hw), F32), jnp.full((1, 1), -1.0, F32))
@@ -126,49 +140,123 @@
     def to_lanes(column):
         return jnp.sum(of_head * column, axis=0, keepdims=True)
 
-    def widen(value):
-        parts = jnp.concatenate([p.astype(F32) for p in three_parts(value)], axis=0)
-        return dot_tn(parts.astype(BF16), spread3)
+    def stacked_parts(value):
+        return jnp.concatenate([p.astype(F32) for p in three_parts(value)], axis=0).astype(BF16)
 
     def stacked_dot(value, right):
-        parts = jnp.concatenate([p.astype(F32) for p in three_parts(value)], axis=0)
-        made = dot_nn(parts.astype(BF16), right)
-        return made[:heads] + made[heads:2 * heads] + made[2 * heads:]
+        made = dot_nn(stacked_parts(value), right)
+        count = value.shape[0]
+        return made[:count] + made[count:2 * count] + made[2 * count:]
+
+    all_steps = jnp.concatenate([step_ref[:, c * q:(c + 1) * q] for c in range(chunks)], axis=0)
+    all_rates = jnp.concatenate([rate] * chunks, axis=0)
+    decay = stacked_dot(-all_steps * all_rates, (square_rows <= square_cols).astype(F32).astype(BF16))
+    whole = decay[:, q - 1:q]
+    from_middle = decay - 0.5 * whole
+    grow, shrink = jnp.exp(from_middle), jnp.exp(-from_middle) * all_steps
+    grows[...], shrinks[...] = grow, shrink
+    total = jnp.zeros((heads, 1), F32)
+    for c in range(chunks):
+        of_chunk = slice(c * heads, (c + 1) * heads)
+        u_parts[c] = stacked_parts(grow[of_chunk])
+        v_parts[c] = stacked_parts(shrink[of_chunk])
+        half[c:c + 1, :] = to_lanes(jnp.exp(0.5 * whole[of_chunk]))
+        phi_f[c:c + 1, :] = to_lanes(jnp.exp(total))
+        total = total + whole[of_chunk]
 
     state[0] = jnp.zeros((states, width), F32)
     back[chunks] = jnp.zeros((states, width), F32)
 
-    def local_states(c, total):
+    def local_states(c):
         rows = rows_of(c)
-        steps = step_ref[:, rows]
-        upper = (square_rows <= square_cols).astype(F32).astype(BF16)
-        decay = stacked_dot(-steps * rate, upper)
-        whole = decay[:, q - 1:q]
-        middle = 0.5 * whole
-        g_scaled = g_ref[rows, :].astype(F32) * widen(jnp.exp(decay - middle))
-        high, low = two_parts(g_scaled)
+        for copy in arrivals(c):
+            copy.wait()
+        high, low = two_parts(g_ref[rows, :].astype(F32) * dot_tn(u_parts[c], spread3))
         ghi[rows, :], glo[rows, :] = high, low
-        x_scale = widen(jnp.exp(middle - decay) * steps)
+        x_scale = dot_tn(v_parts[c], spread3)
         scale[rows, :] = x_scale
         xh, xl = two_parts(x_ref[rows, :].astype(F32) * x_scale)
         xhi[rows, :], xlo[rows, :] = xh, xl
         docs = doc_row(c)
         column = jnp.transpose(jnp.broadcast_to(docs, (lanes, q)))
         doc_col[rows, :] = column
-        half_row = to_lanes(jnp.exp(middle))
-        half[pl.ds(c, 1), :] = half_row
+        half_row = half[pl.ds(c, 1), :]
         w_last = jnp.where(column == docs[:, q - 1:], w_ref[rows, :].astype(F32), 0.0).astype(BF16)
         r_first = jnp.where(column == docs[:, :1], r_ref[rows, :].astype(F32), 0.0).astype(BF16)
         made = (dot_tn(w_last, xh) + dot_tn(w_last, xl)) * half_row
         before = last_doc(jnp.maximum(c - 1, 0))
         kept = jnp.where(before == docs[:, q - 1:], half_row * half_row, 0.0)
         state[c + 1] = made + kept * state[c]
-        back[c] = (dot_tn(r_first, high) + dot_tn(r_first, low)) * half_row
-        phi_f[pl.ds(c, 1), :] = to_lanes(jnp.exp(total))
-        return total + whole
-
-    total = lax.fori_loop(0, chunks, local_states, jnp.zeros((heads, 1), F32))
+        made = (dot_tn(r_first, high) + dot_tn(r_first, low)) * half_row
+        back[c] = made
+        reached = jnp.where(docs[:, :1] == first_doc(0), phi_f[pl.ds(c, 1), :], 0.0)
+        entry[...] = jnp.where(c == 0, made, entry[...] + reached * made)
+
+    pl.loop(0, chunks, unroll=2)(local_states)
     phi_f[pl.ds(chunks, 1), :] = to_lanes(jnp.exp(total))
+    whole_row = to_lanes(total)
+    first_here, last_here = first_doc(0), last_doc(chunks - 1)
+
+    def span_of(ref, which):
+        return ref[which, states:states + 1, :]
+
+    def doc_of(ref, which):
+        return ref[which, states + 1:states + 2, :]
+
+    def value_of(ref, which):
+        return ref[which, 0:states, :]
+
+    def joined(near, near_doc, near_span, far, far_doc):
+        return near + jnp.where(near_doc == far_doc, jnp.exp(near_span), 0.0) * far
+
+    def sib_copy(k, src, dst, ss, rs):
+        return pltpu.make_async_remote_copy(
+            src_ref=src, dst_ref=dst, send_sem=ss.at[k], recv_sem=rs.at[k], device_id=sibling
+        )
+
+    def z_copy(k, far):
+        src, dst, to = (f_out, f_in, me_z + far) if k == 0 else (k_out, k_in, me_z - far)
+        return pltpu.make_async_remote_copy(
+            src_ref=src.at[0], dst_ref=dst.at[far - 1], send_sem=z_ss.at[k, far - 1],
+            recv_sem=z_rs.at[k, far - 1], device_id=at_z(to),
+        )
+
+    def same_doc(c, rows):
+        return jnp.concatenate([doc_col[rows, :]] * doc_rows, axis=1) == doc_row(c)
+
+    def pairs(c):
+        rows = rows_of(c)
+        reads, writes = r_ref[rows, :], w_ref[rows, :]
+        lower = same_doc(c, rows) & (square_rows >= square_cols)
+        xh, xl, gh, gl = xhi[rows, :], xlo[rows, :], ghi[rows, :], glo[rows, :]
+        made = dot_nt(gh, xh) + dot_nt(gh, xl) + dot_nt(gl, xh)
+        high, low = two_parts(jnp.where(lower, made, 0.0))
+        r_acc[rows, :] = dot_nn(high, writes) + dot_nn(low, writes)
+        w_acc[rows, :] = jnp.transpose(dot_tn(reads, high) + dot_tn(reads, low))
+
+    def within(c):
+        rows = rows_of(c)
+        reads, writes = r_ref[rows, :], w_ref[rows, :]
+        same = same_doc(c, rows)
+        lower = same & (square_rows >= square_cols)
+        upper = same & (square_rows <= square_cols)
+        xh, xl, gh, gl = xhi[rows, :], xlo[rows, :], ghi[rows, :], glo[rows, :]
+        high, low = two_parts(jnp.where(lower, dot_nt(reads, writes), 0.0))
+        out_acc[rows, :] = dot_nn(high, xh) + dot_nn(high, xl) + dot_nn(low, xh)
+        high, low = two_parts(jnp.where(upper, dot_nt(writes, reads), 0.0))
+        val_acc[rows, :] = dot_nn(high, gh) + dot_nn(high, gl) + dot_nn(low, gh)
+
+    for k in range(2):
+        lane = slice(k * hw, (k + 1) * hw)
+        put(e_out, k, state[chunks][:, lane], whole_row[:, lane], last_here)
+        put(b_out, k, entry[:, lane], whole_row[:, lane], first_here)
+    pl.semaphore_wait(barrier, 1 + n_z - 1 + 2 * (side - 1))
+    sib_copies = (
+        sib_copy(0, e_out.at[1 - core], e_sib.at[0], sib_ss, sib_rs),
+        sib_copy(1, b_out.at[1 - core], b_sib.at[0], sib_ss, sib_rs),
+    )
+    for copy in sib_copies:
+        copy.start()
     phi_b[pl.ds(chunks, 1), :] = jnp.ones((1, width), F32)
 
     @pl.loop(0, chunks)
@@ -180,65 +268,7 @@
         back[c] = back[c] + kept * back[c + 1]
         phi_b[pl.ds(c, 1), :] = phi_b[pl.ds(c + 1, 1), :] * square
 
-    whole_row = to_lanes(total)
-    first_here, last_here = first_doc(0), last_doc(chunks - 1)
-
-    def span_of(ref, which):
-        return ref[which, states:states + 1, :]
-
-    def doc_of(ref, which):
-        return ref[which, states + 1:states + 2, :]
-
-    def value_of(ref, which):
-        return ref[which, 0:states, :]
-
-    def joined(near, near_doc, near_span, far, far_doc):
-        return near + jnp.where(near_doc == far_doc, jnp.exp(near_span), 0.0) * far
-
-    def sib_copy(k, src, dst, ss, rs):
-        return pltpu.make_async_remote_copy(
-            src_ref=src, dst_ref=dst, send_sem=ss.at[k], recv_sem=rs.at[k], device_id=sibling
-        )
-
-    def z_copy(k, far):
-        src, dst, to = (f_out, f_in, me_z + far) if k == 0 else (k_out, k_in, me_z - far)
-        return pltpu.make_async_remote_copy(
-            src_ref=src.at[0], dst_ref=dst.at[far - 1], send_sem=z_ss.at[k, far - 1],
-            recv_sem=z_rs.at[k, far - 1], device_id=at_z(to),
-        )
-
-    def intra(c):
-        rows = rows_of(c)
-        reads, writes = r_ref[rows, :], w_ref[rows, :]
-        column = doc_col[rows, :]
-        same = jnp.concatenate([column] * doc_rows, axis=1) == doc_row(c)
-        lower = same & (square_rows >= square_cols)
-        upper = same & (square_rows <= square_cols)
-        xh, xl, gh, gl = xhi[rows, :], xlo[rows, :], ghi[rows, :], glo[rows, :]
-        high, low = two_parts(jnp.where(lower, dot_nt(reads, writes), 0.0))
-        out_acc[rows, :] = dot_nn(high, xh) + dot_nn(high, xl) + dot_nn(low, xh)
-        high, low = two_parts(jnp.where(upper, dot_nt(writes, reads), 0.0))
-        val_acc[rows, :] = dot_nn(high, gh) + dot_nn(high, gl) + dot_nn(low, gh)
-        pairs = dot_nt(gh, xh) + dot_nt(gh, xl) + dot_nt(gl, xh)
-        high, low = two_parts(jnp.where(lower, pairs, 0.0))
-        to_read = dot_nn(high, writes) + dot_nn(low, writes)
-        to_write = dot_tn(high, reads) + dot_tn(low, reads)
-        r_acc[rows, :] = to_read
-        w_acc[rows, :] = to_write
-
-    for k in range(2):
-        lane = slice(k * hw, (k + 1) * hw)
-        put(e_out, k, state[chunks][:, lane], whole_row[:, lane], last_here)
-        put(b_out, k, back[0][:, lane], whole_row[:, lane], first_here)
-    pl.semaphore_wait(barrier, 1 + n_z - 1 + 2 * (side - 1))
-    sib_copies = (
-        sib_copy(0, e_out.at[1 - core], e_sib.at[0], sib_ss, sib_rs),
-        sib_copy(1, b_out.at[1 - core], b_sib.at[0], sib_ss, sib_rs),
-    )
-    for copy in sib_copies:
-        copy.start()
-    cuts = (0, chunks // 8, (7 * chunks) // 8, chunks)
-    pl.loop(cuts[0], cuts[1])(intra)
+    first, early = chunks // 8, (3 * chunks) // 8
     for copy in sib_copies:
         copy.wait()
     low, mine, other = core == 0, core, 0
@@ -265,7 +295,8 @@
             def _():
                 z_copy(1, far).start()
 
-    pl.loop(cuts[1], cuts[2], unroll=2)(intra)
+    pl.loop(0, chunks)(pairs)
+    pl.loop(first, early)(within)
     for far in (1, 2):
         if far < n_z:
 
@@ -295,7 +326,7 @@
         copy.start()
     put(s_in, mine, jnp.where(low, s_chip, s_high), span_low, jnp.where(low, s_doc_low, s_doc_high))
     put(g_in, mine, jnp.where(low, g_low, g_chip), span_low, jnp.where(low, g_doc_low, g_doc_high))
-    pl.loop(cuts[2], cuts[3])(intra)
+    pl.loop(0, first)(within)
     for copy in last_copies:
         copy.wait()
 
@@ -318,18 +349,37 @@
     def span_rows(start, count):
         return pl.ds(pl.multiple_of(start, count), count)
 
-    def r_copy(o):
-        x = mod(me_x + o, side)
-        return pltpu.make_async_remote_copy(
-            src_ref=r_acc.at[span_rows(x * group, group)], dst_ref=r_in.at[o - 1],
-            send_sem=r_ss.at[o - 1], recv_sem=r_rs.at[o - 1], device_id=at_xy(x, me_y),
-        )
-
-    def w_copy(o, x):
-        y = mod(me_y + o, side)
-        return pltpu.make_async_remote_copy(
-            src_ref=w_acc.at[span_rows((x * side + y) * block, block)], dst_ref=w_in.at[o - 1, x],
-            send_sem=w_ss.at[o - 1, x], recv_sem=w_rs.at[o - 1, x], device_id=at_xy(me_x, y),
+    def to_side(near):
+        return side - 1 if near else 1
+
+    def r_relay(near):
+        start = mod(me_x + side // 2, side) * group + near * (group // 2)
+        return pltpu.make_async_remote_copy(
+            src_ref=r_acc.at[span_rows(start, group // 2)], dst_ref=r_mid.at[near],
+            send_sem=ra_ss.at[near], recv_sem=ra_rs.at[near],
+            device_id=at_xy(mod(me_x + to_side(near), side), me_y),
+        )
+
+    def r_copy(near):
+        x = mod(me_x + to_side(near), side)
+        return pltpu.make_async_remote_copy(
+            src_ref=r_acc.at[span_rows(x * group, group)], dst_ref=r_in.at[near],
+            send_sem=r_ss.at[near], recv_sem=r_rs.at[near], device_id=at_xy(x, me_y),
+        )
+
+    def w_relay(near, x):
+        start = (x * side + mod(me_y + side // 2, side)) * block + near * (block // 2)
+        return pltpu.make_async_remote_copy(
+            src_ref=w_acc.at[span_rows(start, block // 2)], dst_ref=w_mid.at[near, x],
+            send_sem=wa_ss.at[near, x], recv_sem=wa_rs.at[near, x],
+            device_id=at_xy(me_x, mod(me_y + to_side(near), side)),
+        )
+
+    def w_copy(near, x):
+        y = mod(me_y + to_side(near), side)
+        return pltpu.make_async_remote_copy(
+            src_ref=w_acc.at[span_rows((x * side + y) * block, block)], dst_ref=w_in.at[near, x],
+            send_sem=w_ss.at[near, x], recv_sem=w_rs.at[near, x], device_id=at_xy(me_x, y),
         )
 
     def r_copy2(o):
@@ -355,24 +405,34 @@
         sphi[c], splo[c] = sh, sl
         bh, bl = two_parts(back_at(c + 1, after) * half_row)
         bphi[c], bplo[c] = bh, bl
-        to_read = dot_nt(ghi[rows, :], sh) + dot_nt(ghi[rows, :], sl) + dot_nt(glo[rows, :], sh)
-        to_write = dot_nt(xhi[rows, :], bh) + dot_nt(xhi[rows, :], bl) + dot_nt(xlo[rows, :], bh)
+        pair = dot_nt(ghi[rows, :], jnp.concatenate([sh, sl], axis=0))
+        to_read = pair[:, :states] + pair[:, states:] + dot_nt(glo[rows, :], sh)
+        pair = dot_nt(xhi[rows, :], jnp.concatenate([bh, bl], axis=0))
+        to_write = pair[:, :states] + pair[:, states:] + dot_nt(xlo[rows, :], bh)
         to_read = jnp.where(column == before, to_read, 0.0)
         to_write = jnp.where(column == after, to_write, 0.0)
         r_acc[rows, :] += to_read
         w_acc[rows, :] += to_write
 
+    both = (0, 1)
+
     @pl.loop(0, side)
     def _(i):
-        x = mod(me_x + 1 + i, side)
+        o = jnp.where(i == 0, side // 2, jnp.where(i == 1, 1, jnp.where(i == 2, side - 1, 0)))
+        x = mod(me_x + o, side)
         pl.loop(0, chunks // side, unroll=True)(lambda k: key_grads(x * (chunks // side) + k))
 
-        @pl.when(i < side - 1)
+        @pl.when(i == 0)
         def _():
-            r_copy(i + 1).start()
-
-        for o in range(1, side):
-            w_copy(o, x).start()
+            for near in both:
+                r_relay(near).start()
+
+        for near in both:
+            w_relay(near, x).start()
+
+    def per_head(value):
+        high, low = two_parts(value)
+        return dot_nt(of_head16, high) + dot_nt(of_head16, low)
 
     def rest(c):
         rows = rows_of(c)
@@ -381,15 +441,12 @@
         before, after, last = previous_doc(c), next_doc(c), docs[:, q - 1:]
         reads = jnp.where(column == before, r_ref[rows, :].astype(F32), 0.0).astype(BF16)
         writes = jnp.where(column == after, w_ref[rows, :].astype(F32), 0.0).astype(BF16)
-        out = out_acc[rows, :] + dot_nn(reads, sphi[c]) + dot_nn(reads, splo[c])
-        val = val_acc[rows, :] + dot_nn(writes, bphi[c]) + dot_nn(writes, bplo[c])
+        out = out_acc[rows, :] + dot_nn(jnp.concatenate([reads, reads], axis=1), jnp.concatenate([sphi[c], splo[c]], axis=0))
+        val = val_acc[rows, :] + dot_nn(jnp.concatenate([writes, writes], axis=1), jnp.concatenate([bphi[c], bplo[c]], axis=0))
         vg_ref[rows, :] = (scale[rows, :] * val).astype(BF16)
-        g_scaled = ghi[rows, :].astype(F32) + glo[rows, :].astype(F32)
-        x_scaled = xhi[rows, :].astype(F32) + xlo[rows, :].astype(F32)
-        high, low = two_parts(x_scaled * val)
-        at_write = dot_nt(of_head16, high) + dot_nt(of_head16, low)
-        high, low = two_parts(g_scaled * out)
-        at_read = dot_nt(of_head16, high) + dot_nt(of_head16, low)
+        of_chunk = pl.ds(pl.multiple_of(c * heads, heads), heads)
+        at_write = shrinks[of_chunk, :] * per_head(x_ref[rows, :].astype(F32) * val)
+        at_read = grows[of_chunk, :] * per_head(g_ref[rows, :].astype(F32) * out)
         lower = (jnp.concatenate([column] * doc_rows, axis=1) == docs) & (square_rows >= square_cols)
         later = stacked_dot(at_read - at_write, lower.astype(F32).astype(BF16))
         crossing = jnp.sum(state_at(c + 1, last) * back_at(c + 1, after), axis=0, keepdims=True)
@@ -398,20 +455,40 @@
         later = later + jnp.where(docs == last, crossing, 0.0)
         sg_ref[:, rows] = at_write / step_ref[:, rows] - rate * later
 
-    later_from = (5 * chunks) // 8
-    pl.loop(0, later_from)(rest)
-    for o in range(1, side):
-        r_copy(o).wait_recv()
-
-        @pl.loop(0, side)
-        def _(x):
-            w_copy(o, x).wait_recv()
+    middle_at, late = (4 * chunks) // 8, (5 * chunks) // 8
+    pl.loop(early, middle_at)(within)
+    for near in both:
+        r_relay(near).wait_recv()
+        rows = span_rows(mod(me_x + to_side(near), side) * group + near * (group // 2), group // 2)
+        r_acc[rows, :] += r_mid[near]
+        r_copy(near).start()
+    pl.loop(middle_at, late)(within)
+
+    @pl.loop(0, side)
+    def _(x):
+        for near in both:
+            w_relay(near, x).wait_recv()
+            start = (x * side + mod(me_y + to_side(near), side)) * block + near * (block // 2)
+            rows = span_rows(start, block // 2)
+            w_acc[rows, :] += w_mid[near, x]
+            w_copy(near, x).start()
+
+    pl.loop(late, chunks)(within)
+    later_from = chunks // 2
+    pl.loop(0, later_from, unroll=2)(rest)
+    for near in both:
+        r_copy(near).wait_recv()
+
+    @pl.loop(0, side)
+    def _(x):
+        for near in both:
+            w_copy(near, x).wait_recv()
 
     for o in range(side):
         y = mod(me_y + o, side)
         rows = span_rows((me_x * side + y) * block, block)
         held = r_acc[rows, :]
-        for k in range(side - 1):
+        for k in both:
             held = held + r_in[k, span_rows(y * block, block), :]
         r_acc[rows, :] = held
         if o > 0:
@@ -419,12 +496,12 @@
         x = mod(me_x + o, side)
         rows = span_rows((x * side + me_y) * block, block)
         held = w_acc[rows, :]
-        for k in range(side - 1):
+        for k in both:
             held = held + w_in[k, x]
         w_acc[rows, :] = held
         if o > 0:
             w_copy2(o).start()
-    pl.loop(later_from, chunks)(rest)
+    pl.loop(later_from, chunks, unroll=2)(rest)
     mine_rows = span_rows(me * block, block)
     read_total, write_total = r_acc[mine_rows, :], w_acc[mine_rows, :]
     for o in range(1, side):
@@ -445,14 +522,19 @@
             def _():
                 z_copy(1, far).wait_send()
 
+    for near in both:
+        r_relay(near).wait_send()
+        r_copy(near).wait_send()
+
+    @pl.loop(0, side)
+    def _(x):
+        for near in both:
+            w_relay(near, x).wait_send()
+            w_copy(near, x).wait_send()
+
     for o in range(1, side):
-        r_copy(o).wait_send()
         r_copy2(o).wait_send()
         w_copy2(o).wait_send()
-
-        @pl.loop(0, side)
-        def _(x):
-            w_copy(o, x).wait_send()
 
 
 def shards(mesh_shape, values, step_sizes, decay_rates, write_keys, read_keys, doc_ids, out_grad):
@@ -463,7 +545,7 @@
     chunks = length // QCHUNK
     block = length // n_head
     side = math.isqrt(n_head)
-    vmem = pl.BlockSpec(memory_space=pltpu.VMEM)
+    vmem, hbm = pl.BlockSpec(memory_space=pltpu.VMEM), pl.BlockSpec(memory_space=pl.ANY)
     wide16 = pltpu.VMEM((length, width), BF16)
     wide32 = pltpu.VMEM((length, width), F32)
     def messages(count):
@@ -476,20 +558,27 @@
     value_grad, step_grad, write_grad, read_grad = pl.pallas_call(
         partial(kernel, n_ctx, n_head),
         out_shape=(
-            jax.ShapeDtypeStruct((length, width), BF16),
-            jax.ShapeDtypeStruct((heads, length), F32),
-            jax.ShapeDtypeStruct((block, states), F32),
-            jax.ShapeDtypeStruct((block, states), F32),
+            pltpu.VMEM((length, width), BF16),
+            pltpu.VMEM((heads, length), F32),
+            pltpu.VMEM((block, states), F32),
+            pltpu.VMEM((block, states), F32),
         ),
-        in_specs=[vmem, vmem, vmem, pl.BlockSpec(memory_space=pltpu.SMEM), vmem, vmem, vmem],
+        in_specs=[hbm, hbm, vmem, pl.BlockSpec(memory_space=pltpu.SMEM), hbm, hbm, vmem],
         out_specs=(vmem, vmem, vmem, vmem),
         scratch_shapes=[
+            wide16, wide16, pltpu.VMEM((length, states), BF16), pltpu.VMEM((length, states), BF16),
+            pltpu.SemaphoreType.DMA((4, chunks)),
+            pltpu.VMEM((chunks, 3 * heads, QCHUNK), BF16), pltpu.VMEM((chunks, 3 * heads, QCHUNK), BF16),
+            pltpu.VMEM((chunks * heads, QCHUNK), F32), pltpu.VMEM((chunks * heads, QCHUNK), F32),
+            pltpu.VMEM((states, width), F32),
             wide16, wide16, wide16, wide16, wide32, wide32, wide32,
             pltpu.VMEM((length, 128), F32),
             pltpu.VMEM((length, states), F32),
             pltpu.VMEM((length, states), F32),
-            pltpu.VMEM((others, length // side, states), F32),
-            pltpu.VMEM((others, side, block, states), F32),
+            pltpu.VMEM((2, length // side // 2, states), F32),
+            pltpu.VMEM((2, side, block // 2, states), F32),
+            pltpu.VMEM((2, length // side, states), F32),
+            pltpu.VMEM((2, side, block, states), F32),
             pltpu.VMEM((others, block, states), F32),
             pltpu.VMEM((others, block, states), F32),
             pltpu.VMEM((chunks + 1, states, width), F32),
@@ -504,10 +593,11 @@
             messages(2), messages(2), messages(1), messages(1), messages(1), messages(1),
             messages(2), messages(2), messages(1), messages(1), messages(2), messages(2),
             *semaphores(2), *semaphores(2, 2), *semaphores(2),
-            *semaphores(others), *semaphores(others, side), *semaphores(others), *semaphores(others),
+            *semaphores(2), *semaphores(2, side), *semaphores(2), *semaphores(2, side),
+            *semaphores(others), *semaphores(others),
         ],
         compiler_params=pltpu.CompilerParams(
-            collective_id=0, has_side_effects=True, vmem_limit_bytes=60 * 2**20
+            collective_id=0, has_side_effects=True, vmem_limit_bytes=58 * 2**20
         ),
     )(
         values, out_grad, step_sizes.T, decay_rates, write_keys, read_keys,

time: 56.1 us -> 48.7 us (0.87); the launches traced: 55.2 us -> 48.6 us
  Pallas kernels: 49.5 us -> 44.7 us
  local copies, waits for them, and re-layouts: 4.99 us -> 3.21 us
    pallas_call x1, Pallas kernels: 49.5 us -> 44.7 us  [shards(): pl.pallas_call(partial(kernel, n_ctx, n_head), out_shape=(pltpu.VMEM((len...]
    unnamed x10 -> x4, local copies, waits for them, and re-layouts: 4.99 us -> 3.21 us
where the time goes in v3:
time: 48.7 us; the launch traced here: 48.6 us
  Pallas kernels  44.7 us (92%)
  local copies, waits for them, and re-layouts  3.21 us (7%)
  between operations  0.64 us (1%)
    pallas_call x1, Pallas kernels, shards(): pl.pallas_call(partial(kernel, n_ctx, n_head), out_shape=(pltpu.VMEM((len...  44.7 us
    unnamed x4, local copies, waits for them, and re-layouts  3.21 us

profile of v3, /device:TPU:0, one launch (start us, length us, event | category | flops | bytes accessed | tf_op | source)
XLA Modules:
  0.0 48.6 jit_solution(4995675420717377683)
XLA Ops:
  0.6 44.7 %shard_map.102 = (bf16[2048,512]{1,0:T(8,128)(2,1)S(1)}, f32[8,2048]{1,0:T(8,128)S(1)}, f32[128,128]{1,0:T(8,128)S(1)}, f32[128,128]{1,0:T(8,128)S(1)}) custom-call(bf16[2048,512]{1,0:T(8,128)(2,1)} %x_hbm.1, bf16[2048,512]{1,0:T(8,128)(2,1)} %g_hbm.1, f32[8,2048]{1,0:T(8,128)} %bitcast.4, f32[8]{0:T(128)} %rate_ref.1, bf16[2048,128]{1,0:T(8,128)(2,1)} %w_hbm.1, ...), custom_call_target="tpu_custom_call" | custom-call | tf_op jit(solution)/shard_map/pallas_call | solution.py:558
  45.3 1.3 %copy.15 = bf16[2048,512]{1,0:T(8,128)(2,1)} copy(bf16[2048,512]{1,0:T(8,128)(2,1)S(1)} %get-tuple-element.12) | data formatting | bytes 4194304
  46.7 0.6 %copy.16 = f32[2048,8]{0,1:T(8,128)} copy(f32[2048,8]{0,1:T(8,128)S(1)} %bitcast.3) | data formatting | bytes 131072
  47.3 0.6 %copy.17 = f32[128,128]{1,0:T(8,128)} copy(f32[128,128]{1,0:T(8,128)S(1)} %get-tuple-element.14) | data formatting | bytes 131072
  47.9 0.6 %copy.18 = f32[128,128]{1,0:T(8,128)} copy(f32[128,128]{1,0:T(8,128)S(1)} %get-tuple-element.15) | data formatting | bytes 131072

commit v4 on v3

--- a/solution.py
+++ b/solution.py
@@ -46,9 +46,9 @@
 
 
 def kernel(
-    n_ctx, n_head, x_hbm, g_hbm, step_ref, rate_ref, w_hbm, r_hbm, doc_ref,
-    vg_ref, sg_ref, wg_ref, rg_ref,
-    x_ref, g_ref, w_ref, r_ref, in_sems, u_parts, v_parts, grows, shrinks, entry,
+    n_ctx, n_head, x_hbm, g_hbm, step_hbm, rate_ref, w_hbm, r_hbm, doc_hbm,
+    vg_ref, sg_ref, kg_ref,
+    x_ref, g_ref, w_ref, r_ref, step_ref, doc_ref, small_sems, in_sems, u_parts, v_parts, grows, shrinks, entry,
     xhi, xlo, ghi, glo, scale, out_acc, val_acc, doc_col,
     r_acc, w_acc, r_mid, w_mid, r_in, w_in, r_in2, w_in2,
     state, back, half, phi_f, phi_b, sphi, splo, bphi, bplo,
@@ -57,7 +57,7 @@
     ra_ss, ra_rs, wa_ss, wa_rs, r_ss, r_rs, w_ss, w_rs, r2_ss, r2_rs, w2_ss, w2_rs,
 ):
     length, width = x_hbm.shape
-    heads = step_ref.shape[0]
+    heads = step_hbm.shape[0]
     head_size = width // heads
     states = w_hbm.shape[1]
     q = QCHUNK
@@ -94,6 +94,13 @@
             for k, (src, dst) in enumerate(pairs)
         ]
 
+    small = (
+        pltpu.make_async_copy(step_hbm, step_ref, small_sems.at[0]),
+        pltpu.make_async_copy(doc_hbm, doc_ref, small_sems.at[1]),
+    )
+    for copy in small:
+        copy.start()
+
     @pl.loop(0, chunks)
     def _(c):
         for copy in arrivals(c):
@@ -148,6 +155,8 @@
         count = value.shape[0]
         return made[:count] + made[count:2 * count] + made[2 * count:]
 
+    for copy in small:
+        copy.wait()
     all_steps = jnp.concatenate([step_ref[:, c * q:(c + 1) * q] for c in range(chunks)], axis=0)
     all_rates = jnp.concatenate([rate] * chunks, axis=0)
     decay = stacked_dot(-all_steps * all_rates, (square_rows <= square_cols).astype(F32).astype(BF16))
@@ -509,8 +518,8 @@
         read_total = read_total + r_in2[o - 1]
         w_copy2(o).wait_recv()
         write_total = write_total + w_in2[o - 1]
-    wg_ref[...] = write_total
-    rg_ref[...] = read_total
+    kg_ref[0] = -write_total
+    kg_ref[1] = -read_total
     for far in (1, 2):
         if far < n_z:
 
@@ -555,19 +564,19 @@
         return [pltpu.SemaphoreType.DMA(shape)] * 2
 
     others = max(side - 1, 1)
-    value_grad, step_grad, write_grad, read_grad = pl.pallas_call(
+    value_grad, step_grad, key_grad = pl.pallas_call(
         partial(kernel, n_ctx, n_head),
         out_shape=(
             pltpu.VMEM((length, width), BF16),
             pltpu.VMEM((heads, length), F32),
-            pltpu.VMEM((block, states), F32),
-            pltpu.VMEM((block, states), F32),
+            pltpu.VMEM((2, block, states), F32),
         ),
-        in_specs=[hbm, hbm, vmem, pl.BlockSpec(memory_space=pltpu.SMEM), hbm, hbm, vmem],
-        out_specs=(vmem, vmem, vmem, vmem),
+        in_specs=[hbm, hbm, hbm, pl.BlockSpec(memory_space=pltpu.SMEM), hbm, hbm, hbm],
+        out_specs=(vmem, vmem, vmem),
         scratch_shapes=[
             wide16, wide16, pltpu.VMEM((length, states), BF16), pltpu.VMEM((length, states), BF16),
-            pltpu.SemaphoreType.DMA((4, chunks)),
+            pltpu.VMEM((heads, length), F32), pltpu.VMEM((length // 128, 128), jnp.int32),
+            pltpu.SemaphoreType.DMA((2,)), pltpu.SemaphoreType.DMA((4, chunks)),
             pltpu.VMEM((chunks, 3 * heads, QCHUNK), BF16), pltpu.VMEM((chunks, 3 * heads, QCHUNK), BF16),
             pltpu.VMEM((chunks * heads, QCHUNK), F32), pltpu.VMEM((chunks * heads, QCHUNK), F32),
             pltpu.VMEM((states, width), F32),
@@ -603,7 +612,7 @@
         values, out_grad, step_sizes.T, decay_rates, write_keys, read_keys,
         doc_ids.reshape(length // 128, 128),
     )
-    return value_grad, step_grad.T, write_grad, read_grad
+    return value_grad, step_grad.T, -key_grad[0], -key_grad[1]
 
 
 def solution(mesh):

time: 48.7 us -> 48.2 us (0.990)
  local copies, waits for them, and re-layouts: 3.21 us -> 1.95 us
  other arithmetic: 0 us -> 0.66 us
    unnamed x4 -> x2, local copies, waits for them, and re-layouts: 3.21 us -> 1.95 us
    neg x0 -> x1, other arithmetic: none -> 0.66 us  [shards(): return (value_grad, step_grad.T, -key_grad[0], -key_grad[1])]
where the time goes in v4:
time: 48.2 us; the launch traced here: 48 us
  Pallas kernels  44.8 us (93%)
  local copies, waits for them, and re-layouts  1.95 us (4%)
  other arithmetic  0.66 us (1%)
  between operations  0.64 us (1%)
    pallas_call x1, Pallas kernels, shards(): pl.pallas_call(partial(kernel, n_ctx, n_head), out_shape=(pltpu.VMEM((len...  44.8 us
    unnamed x2, local copies, waits for them, and re-layouts  1.95 us

profile of v4, /device:TPU:0, one launch (start us, length us, event | category | flops | bytes accessed | tf_op | source)
XLA Modules:
  0.0 48.0 jit_solution(606991125050975664)
XLA Ops:
  0.6 44.8 %shard_map.102 = (bf16[2048,512]{1,0:T(8,128)(2,1)S(1)}, f32[8,2048]{1,0:T(8,128)S(1)}, f32[2,128,128]{2,1,0:T(8,128)S(1)}) custom-call(bf16[2048,512]{1,0:T(8,128)(2,1)} %x_hbm.1, bf16[2048,512]{1,0:T(8,128)(2,1)} %g_hbm.1, f32[8,2048]{1,0:T(8,128)} %bitcast.8, f32[8]{0:T(128)} %rate_ref.1, bf16[2048,128]{1,0:T(8,128)(2,1)} %w_hbm.1, ...), custom_call_target="tpu_custom_call" | custom-call | tf_op jit(solution)/shard_map/pallas_call | solution.py:567
  45.4 1.3 %copy.13 = bf16[2048,512]{1,0:T(8,128)(2,1)} copy(bf16[2048,512]{1,0:T(8,128)(2,1)S(1)} %get-tuple-element.12) | data formatting | bytes 4194304
  46.8 0.6 %copy.14 = f32[2048,8]{0,1:T(8,128)} copy(f32[2048,8]{0,1:T(8,128)S(1)} %bitcast.7) | data formatting | bytes 131072
  47.4 0.7 %negate_bitcast_fusion = (f32[128,128]{1,0:T(8,128)}, f32[128,128]{1,0:T(8,128)}) fusion(f32[2,128,128]{2,1,0:T(8,128)S(1)} %get-tuple-element.9), kind=kLoop, calls=%fused_computation | loop fusion | flops 32768 | bytes 262144 | tf_op jit(solution)/shard_map/neg | solution.py:615

commit v5 on v4

--- a/solution.py
+++ b/solution.py
@@ -47,7 +47,7 @@
 
 def kernel(
     n_ctx, n_head, x_hbm, g_hbm, step_hbm, rate_ref, w_hbm, r_hbm, doc_hbm,
-    vg_ref, sg_ref, kg_ref,
+    vg_ref, kg_ref,
     x_ref, g_ref, w_ref, r_ref, step_ref, doc_ref, small_sems, in_sems, u_parts, v_parts, grows, shrinks, entry,
     xhi, xlo, ghi, glo, scale, out_acc, val_acc, doc_col,
     r_acc, w_acc, r_mid, w_mid, r_in, w_in, r_in2, w_in2,
@@ -462,7 +462,10 @@
         crossing = jnp.sum(of_head * crossing, axis=1, keepdims=True)
         crossing = jnp.where(last == after, crossing, 0.0)
         later = later + jnp.where(docs == last, crossing, 0.0)
-        sg_ref[:, rows] = at_write / step_ref[:, rows] - rate * later
+        step_grad = rate * later - at_write / step_ref[:, rows]
+        for k in range(doc_rows):
+            at = pl.ds(pl.multiple_of((c * doc_rows + k) * heads, heads), heads)
+            kg_ref[2, at, :] = step_grad[:, k * lanes:(k + 1) * lanes]
 
     middle_at, late = (4 * chunks) // 8, (5 * chunks) // 8
     pl.loop(early, middle_at)(within)
@@ -564,15 +567,14 @@
         return [pltpu.SemaphoreType.DMA(shape)] * 2
 
     others = max(side - 1, 1)
-    value_grad, step_grad, key_grad = pl.pallas_call(
+    value_grad, small_grads = pl.pallas_call(
         partial(kernel, n_ctx, n_head),
         out_shape=(
             pltpu.VMEM((length, width), BF16),
-            pltpu.VMEM((heads, length), F32),
-            pltpu.VMEM((2, block, states), F32),
+            pltpu.VMEM((3, block, states), F32),
         ),
         in_specs=[hbm, hbm, hbm, pl.BlockSpec(memory_space=pltpu.SMEM), hbm, hbm, hbm],
-        out_specs=(vmem, vmem, vmem),
+        out_specs=(vmem, vmem),
         scratch_shapes=[
             wide16, wide16, pltpu.VMEM((length, states), BF16), pltpu.VMEM((length, states), BF16),
             pltpu.VMEM((heads, length), F32), pltpu.VMEM((length // 128, 128), jnp.int32),
@@ -612,7 +614,8 @@
         values, out_grad, step_sizes.T, decay_rates, write_keys, read_keys,
         doc_ids.reshape(length // 128, 128),
     )
-    return value_grad, step_grad.T, -key_grad[0], -key_grad[1]
+    step_grad = (-small_grads[2]).reshape(length // 128, heads, 128).transpose(0, 2, 1).reshape(length, heads)
+    return value_grad, step_grad, -small_grads[0], -small_grads[1]
 
 
 def solution(mesh):

time: 48.2 us -> 47.6 us (0.988)
  local copies, waits for them, and re-layouts: 1.95 us -> 1.32 us
    unnamed x2 -> x1, local copies, waits for them, and re-layouts: 1.95 us -> 1.32 us
where the time goes in v5:
time: 47.6 us; the launch traced here: 47.4 us
  Pallas kernels  44.8 us (94%)
  local copies, waits for them, and re-layouts  1.32 us (3%)
  other arithmetic  0.68 us (1%)
  between operations  0.64 us (1%)
    pallas_call x1, Pallas kernels, shards(): pl.pallas_call(partial(kernel, n_ctx, n_head), out_shape=(pltpu.VMEM((len...  44.8 us
    unnamed x1, local copies, waits for them, and re-layouts  1.32 us

profile of v5, /device:TPU:0, one launch (start us, length us, event | category | flops | bytes accessed | tf_op | source)
XLA Modules:
  0.0 47.4 jit_solution(13548829435574155645)
XLA Ops:
  0.6 44.8 %shard_map.102 = (bf16[2048,512]{1,0:T(8,128)(2,1)S(1)}, f32[3,128,128]{2,1,0:T(8,128)S(1)}) custom-call(bf16[2048,512]{1,0:T(8,128)(2,1)} %x_hbm.1, bf16[2048,512]{1,0:T(8,128)(2,1)} %g_hbm.1, f32[8,2048]{1,0:T(8,128)} %bitcast.12, f32[8]{0:T(128)} %rate_ref.1, bf16[2048,128]{1,0:T(8,128)(2,1)} %w_hbm.1, bf16[2048,128]{1,0:T(8,128)(2,1)} %r_hbm.1, ...), custom_call_target="tpu_custom_call" | custom-call | tf_op jit(solution)/shard_map/pallas_call | solution.py:570
  45.4 1.3 %copy.12 = bf16[2048,512]{1,0:T(8,128)(2,1)} copy(bf16[2048,512]{1,0:T(8,128)(2,1)S(1)} %get-tuple-element.11) | data formatting | bytes 4194304
  46.8 0.7 %negate_bitcast_fusion = (f32[128,128]{1,0:T(8,128)}, f32[128,128]{1,0:T(8,128)}, f32[2048,8]{0,1:T(8,128)}) fusion(f32[3,128,128]{2,1,0:T(8,128)S(1)} %get-tuple-element.7), kind=kLoop, calls=%fused_computation | loop fusion | flops 49152 | bytes 393216 | tf_op jit(solution)/shard_map/neg | solution.py:618
